TPU v7x, 32 devices: a whole 2x2x4 slice. The times are simulated.
32 devices in a mesh: section: 2 (over y), dp: 16 (over z, x, core).
Axes of the slice: x: 2, y: 2, z: 4, core: 2. Of those that a mesh axis runs over, the one named last changes fastest.
Arguments:
- tokens: bfloat16 [2, 4096, 576], P(None, 'dp'), may hold values from -6 to 6
- segments: int32 [2, 16, 256], P(None, 'dp'), may hold values from 0 to 3, never falling along the last dimension, each value on 1 to 128 neighbouring positions
- w_query: bfloat16 [2, 331776], P('section', 'dp'), may hold values from -0.375 to 0.375
- w_key: bfloat16 [2, 110592], P('section', 'dp'), may hold values from -0.375 to 0.375
- w_value: bfloat16 [2, 110592], P('section', 'dp'), may hold values from -0.25 to 0.25
- w_out: bfloat16 [2, 331776], P('section', 'dp'), may hold values from -0.75 to 0.75
- w_gate: bfloat16 [2, 884736], P('section', 'dp'), may hold values from -0.25 to 0.25
- w_up: bfloat16 [2, 884736], P('section', 'dp'), may hold values from -0.25 to 0.25
- w_down: bfloat16 [2, 884736], P('section', 'dp'), may hold values from -0.15625 to 0.15625
- attn_gain: float32 [2, 576], P('section'), may hold values from 0.5 to 1.5
- mlp_gain: float32 [2, 576], P('section'), may hold values from 0.5 to 1.5
- out_grad: bfloat16 [2, 4096, 576], P(None, 'dp'), may hold values from -6 to 6
Outputs:
- layer_out: bfloat16 [2, 2, 4096, 576], P('section', None, 'dp')
- input_grad: bfloat16 [2, 2, 4096, 576], P('section', None, 'dp')
- grad_w_query: float32 [2, 331776], P('section', 'dp')
- grad_w_key: float32 [2, 110592], P('section', 'dp')
- grad_w_value: float32 [2, 110592], P('section', 'dp')
- grad_w_out: float32 [2, 331776], P('section', 'dp')
- grad_w_gate: float32 [2, 884736], P('section', 'dp')
- grad_w_up: float32 [2, 884736], P('section', 'dp')
- grad_w_down: float32 [2, 884736], P('section', 'dp')
- grad_attn_gain: float32 [2, 576], P('section')
- grad_mlp_gain: float32 [2, 576], P('section')
Inputs may be any that keep to these rules, and one draw needn't show every extreme that they name: `segments`: segment numbers never fall along a pack of 256 tokens; each document (a run of one number) has 1 to 128 tokens.
All inputs are finite; a program needn't handle non-finite values.
Results may differ from a plain program's by a relative error of at most 0.025.
The roundings to bfloat16 on the way count: a program that leaves them out, or rounds other values in their place, can miss the bound.
Values may be sent and summed in bfloat16 or wider, within the bound.
No kernel may reach another device: no remote copies, remote signals or barrier semaphores. Data moves between devices by JAX's collectives and lax.ppermute only.
A program may use at most 128 MiB of HBM per device.

v0:
```python
import math

import jax
import jax.numpy as jnp
from jax import lax
from jax.sharding import PartitionSpec as P

D = 576
HEADS = 9
KV_HEADS = 3
HEAD = 64
FF = 1536
MICRO = 2
TOK_MB = 256


EPS = 1e-05
THETA = 100000.0
NEG = -1000000000.0


def passed_along(block, axis, distance):
    devices = range(lax.axis_size(axis))
    route = [(i - distance, i) for i in devices if i - distance in devices]
    return lax.ppermute(block, axis, route)


def rotate(values):
    half_dim = values.shape[-1] // 2
    return jnp.concatenate([-values[..., half_dim:], values[..., :half_dim]], -1)


def rope(values, cosine, sine_tab):
    return values * cosine + rotate(values) * sine_tab


def rope_back(grads, cosine, sine_tab):
    return grads * cosine - rotate(grads * sine_tab)


def make_tables(seg_row):
    count_t = seg_row.shape[0]
    order_idx = jnp.arange(count_t, dtype=jnp.int32)
    same_doc = seg_row[:, None] == seg_row[None, :]
    before = order_idx[None, :] < order_idx[:, None]
    positions = jnp.sum(jnp.where(same_doc & before, jnp.float32(1.0), jnp.float32(0.0)), axis=1)
    allowed = same_doc & (order_idx[None, :] <= order_idx[:, None])
    inv_freq = jnp.exp(jnp.arange(HEAD // 2, dtype=jnp.float32) * (-2.0 * math.log(THETA) / HEAD))
    angles = positions[:, None] * inv_freq[None, :]
    angles = jnp.concatenate([angles, angles], -1)
    return (jnp.cos(angles)[:, None, :], jnp.sin(angles)[:, None, :], allowed)


def matmul(left, right):
    return jnp.dot(left, right, preferred_element_type=jnp.float32)


def matmul_nt(left, right):
    return jnp.einsum("ta,ba->tb", left, right, preferred_element_type=jnp.float32)


def matmul_tn(left, right):
    return jnp.einsum("ta,tb->ab", left, right, preferred_element_type=jnp.float32)


def inv_rms(stream):
    return lax.rsqrt(jnp.mean(stream * stream, -1, keepdims=True) + EPS)


def norm_back(stream, gain_row, grad_normed):
    scale_r = inv_rms(stream)
    weighted = grad_normed * gain_row
    grad_stream = scale_r * weighted - stream * scale_r**3 * jnp.mean(
        stream * weighted, -1, keepdims=True
    )
    grad_gain = jnp.sum(grad_normed * stream * scale_r, 0)
    return (grad_stream, grad_gain)


def attention_scores(queries, key_rot, allowed):
    scores = jnp.einsum(
        "tkrh,skh->krts", queries, key_rot, preferred_element_type=jnp.float32
    ) * HEAD ** (-0.5)
    return jnp.where(allowed, scores, NEG)


def block_rows(count_t):
    return min(512, count_t)


def layer_forward(stream, matrices, gain_pair, tables):
    w_query, w_key, w_value, w_out, w_gate, w_up, w_down = matrices
    cosine, sine_tab, allowed = tables
    count_t = stream.shape[0]
    repeat = HEADS // KV_HEADS
    block_n = block_rows(count_t)
    blocks = count_t // block_n
    normed_a = (stream * inv_rms(stream) * gain_pair[0]).astype(jnp.bfloat16)
    query_raw = matmul(normed_a, w_query)
    key_raw = matmul(normed_a, w_key)
    value_raw = matmul(normed_a, w_value)
    queries = rope(query_raw.reshape(count_t, HEADS, HEAD), cosine, sine_tab).astype(jnp.bfloat16)
    queries = queries.reshape(count_t, KV_HEADS, repeat, HEAD)
    key_rot = rope(key_raw.reshape(count_t, KV_HEADS, HEAD), cosine, sine_tab).astype(jnp.bfloat16)
    value_low = value_raw.astype(jnp.bfloat16).reshape(count_t, KV_HEADS, HEAD)

    def forward_block(pair):
        query_blk, allow_blk = pair
        scores = attention_scores(query_blk, key_rot, allow_blk)
        row_max = jnp.max(scores, -1, keepdims=True)
        exp_terms = jnp.exp(scores - row_max)
        row_total = jnp.sum(exp_terms, -1, keepdims=True)
        attend = exp_terms / row_total
        mixed_blk = jnp.einsum(
            "krts,skh->tkrh",
            attend.astype(jnp.bfloat16),
            value_low,
            preferred_element_type=jnp.float32,
        )
        return (mixed_blk, row_max + jnp.log(row_total))

    mixed_blocks, log_total = lax.map(
        forward_block,
        (
            queries.reshape(blocks, block_n, KV_HEADS, repeat, HEAD),
            allowed.reshape(blocks, block_n, count_t),
        ),
    )
    mixed_heads = mixed_blocks.reshape(count_t, HEADS * HEAD).astype(jnp.bfloat16)
    middle = stream + matmul(mixed_heads, w_out)
    normed_b = (middle * inv_rms(middle) * gain_pair[1]).astype(jnp.bfloat16)
    gate_raw = matmul(normed_b, w_gate)
    up_raw = matmul(normed_b, w_up)
    activated = (jax.nn.silu(gate_raw) * up_raw).astype(jnp.bfloat16)
    result = middle + matmul(activated, w_down)
    stored = (
        stream,
        normed_a,
        queries,
        key_rot,
        value_low,
        log_total,
        mixed_heads,
        middle,
        normed_b,
        gate_raw,
        up_raw,
        activated,
    )
    return (result, stored)


def layer_backward(grad_out, matrices, gain_pair, tables, stored):
    w_query, w_key, w_value, w_out, w_gate, w_up, w_down = matrices
    cosine, sine_tab, allowed = tables
    (
        stream,
        normed_a,
        queries,
        key_rot,
        value_low,
        log_total,
        mixed_heads,
        middle,
        normed_b,
        gate_raw,
        up_raw,
        activated,
    ) = stored
    count_t = stream.shape[0]
    repeat = HEADS // KV_HEADS
    block_n = block_rows(count_t)
    blocks = count_t // block_n
    grad_mlp = grad_out.astype(jnp.bfloat16)
    grad_act = matmul_nt(grad_mlp, w_down)
    sigmoid_g = jax.nn.sigmoid(gate_raw)
    grad_gate = (grad_act * up_raw * sigmoid_g * (1.0 + gate_raw * (1.0 - sigmoid_g))).astype(
        jnp.bfloat16
    )
    grad_up = (grad_act * gate_raw * sigmoid_g).astype(jnp.bfloat16)
    grad_normed_b = matmul_nt(grad_gate, w_gate) + matmul_nt(grad_up, w_up)
    back_b, gain_grad_b = norm_back(middle, gain_pair[1], grad_normed_b)
    grad_middle = grad_out + back_b
    grad_attn = grad_middle.astype(jnp.bfloat16)
    grad_mixed = (
        matmul_nt(grad_attn, w_out).astype(jnp.bfloat16).reshape(count_t, KV_HEADS, repeat, HEAD)
    )

    def backward_block(carry, inputs):
        value_sum, key_sum = carry
        query_blk, grad_blk, allow_blk, log_blk = inputs
        scores = attention_scores(query_blk, key_rot, allow_blk)
        attend = jnp.exp(scores - log_blk)
        grad_attend = jnp.einsum(
            "tkrh,skh->krts", grad_blk, value_low, preferred_element_type=jnp.float32
        )
        value_sum = value_sum + jnp.einsum(
            "krts,tkrh->skh",
            attend.astype(jnp.bfloat16),
            grad_blk,
            preferred_element_type=jnp.float32,
        )
        inner_sum = jnp.sum(attend * grad_attend, -1, keepdims=True)
        grad_scores = (attend * (grad_attend - inner_sum)).astype(jnp.bfloat16)
        query_part = jnp.einsum(
            "krts,skh->tkrh", grad_scores, key_rot, preferred_element_type=jnp.float32
        ) * HEAD ** (-0.5)
        key_sum = key_sum + jnp.einsum(
            "krts,tkrh->skh", grad_scores, query_blk, preferred_element_type=jnp.float32
        ) * HEAD ** (-0.5)
        return ((value_sum, key_sum), query_part)

    zero_kv = jnp.zeros((count_t, KV_HEADS, HEAD), jnp.float32)
    (grad_value, grad_key), grad_query = lax.scan(
        backward_block,
        (zero_kv, zero_kv),
        (
            queries.reshape(blocks, block_n, KV_HEADS, repeat, HEAD),
            grad_mixed.reshape(blocks, block_n, KV_HEADS, repeat, HEAD),
            allowed.reshape(blocks, block_n, count_t),
            log_total,
        ),
    )
    grad_value = grad_value.astype(jnp.bfloat16).reshape(count_t, KV_HEADS * HEAD)
    grad_query = rope_back(grad_query.reshape(count_t, HEADS, HEAD), cosine, sine_tab)
    grad_query = grad_query.astype(jnp.bfloat16).reshape(count_t, HEADS * HEAD)
    grad_key = (
        rope_back(grad_key, cosine, sine_tab).astype(jnp.bfloat16).reshape(count_t, KV_HEADS * HEAD)
    )
    grad_normed_a = (
        matmul_nt(grad_query, w_query) + matmul_nt(grad_key, w_key) + matmul_nt(grad_value, w_value)
    )
    back_a, gain_grad_a = norm_back(stream, gain_pair[0], grad_normed_a)
    grad_in = grad_middle + back_a
    kept_rows = (
        normed_a,
        grad_query,
        grad_key,
        grad_value,
        mixed_heads,
        grad_attn,
        normed_b,
        grad_gate,
        grad_up,
        activated,
        grad_mlp,
    )
    return (grad_in, kept_rows, jnp.stack([gain_grad_a, gain_grad_b]))


def weight_grads(kept_rows):
    (
        normed_a,
        grad_query,
        grad_key,
        grad_value,
        mixed_heads,
        grad_attn,
        normed_b,
        grad_gate,
        grad_up,
        activated,
        grad_mlp,
    ) = kept_rows
    return (
        matmul_tn(normed_a, grad_query),
        matmul_tn(normed_a, grad_key),
        matmul_tn(normed_a, grad_value),
        matmul_tn(mixed_heads, grad_attn),
        matmul_tn(normed_b, grad_gate),
        matmul_tn(normed_b, grad_up),
        matmul_tn(activated, grad_mlp),
    )


def pick(tree_in, index_at):

    def take(member):
        return lax.dynamic_index_in_dim(member, index_at, 0, keepdims=False)

    return jax.tree.map(take, tree_in)


def stack_slice(entries, start_at, count_m):

    def join(position):
        return lax.dynamic_slice_in_dim(
            jnp.stack([entry[position] for entry in entries]), start_at, count_m, 0
        )

    return tuple((join(position) for position in range(len(entries[0]))))


def shards(
    tokens,
    segments,
    w_query,
    w_key,
    w_value,
    w_out,
    w_gate,
    w_up,
    w_down,
    attn_gain,
    mlp_gain,
    out_grad,
):
    section_no = lax.axis_index("section")
    section_count = lax.axis_size("section")
    owner_count = lax.axis_size("dp")
    tick_count = MICRO + section_count - 1
    mat_shapes = (
        (D, HEADS * HEAD),
        (D, KV_HEADS * HEAD),
        (D, KV_HEADS * HEAD),
        (HEADS * HEAD, D),
        (D, FF),
        (D, FF),
        (FF, D),
    )

    def unpack(gathered):
        return tuple((member.reshape(mat_shape) for member, mat_shape in zip(gathered, mat_shapes)))

    matrices = unpack(
        (
            lax.all_gather(w_query, "dp", axis=0, tiled=True),
            lax.all_gather(w_key, "dp", axis=0, tiled=True),
            lax.all_gather(w_value, "dp", axis=0, tiled=True),
            lax.all_gather(w_out, "dp", axis=0, tiled=True),
            lax.all_gather(w_gate, "dp", axis=0, tiled=True),
            lax.all_gather(w_up, "dp", axis=0, tiled=True),
            lax.all_gather(w_down, "dp", axis=0, tiled=True),
        )
    )
    gain_pair = (attn_gain[0], mlp_gain[0])
    tables_all = jax.vmap(make_tables)(segments[:, 0])
    arrived = jnp.zeros((TOK_MB, D), jnp.bfloat16)
    results = []
    stores = []
    for step_no in range(tick_count):
        micro_idx = jnp.clip(step_no - section_no, 0, MICRO - 1)
        own_rows = lax.dynamic_index_in_dim(tokens, micro_idx, 0, keepdims=False)
        stream_in = jnp.where(section_no == 0, own_rows, arrived).astype(jnp.float32)
        result, stored = layer_forward(stream_in, matrices, gain_pair, pick(tables_all, micro_idx))
        sent_rows = result.astype(jnp.bfloat16)
        results.append(sent_rows)
        stores.append(stored)
        if step_no + 1 < tick_count:
            arrived = passed_along(sent_rows, "section", 1)
    layer_out = lax.dynamic_slice_in_dim(jnp.stack(results), section_no, MICRO, 0)
    stored_all = stack_slice(stores, section_no, MICRO)
    back_mats = unpack(
        (
            lax.all_gather(w_query, "dp", axis=0, tiled=True),
            lax.all_gather(w_key, "dp", axis=0, tiled=True),
            lax.all_gather(w_value, "dp", axis=0, tiled=True),
            lax.all_gather(w_out, "dp", axis=0, tiled=True),
            lax.all_gather(w_gate, "dp", axis=0, tiled=True),
            lax.all_gather(w_up, "dp", axis=0, tiled=True),
            lax.all_gather(w_down, "dp", axis=0, tiled=True),
        )
    )
    delay_by = section_count - 1 - section_no
    arrived_grad = jnp.zeros((TOK_MB, D), jnp.bfloat16)
    grads_in = []
    kept_list = []
    gain_list = []
    for step_no in range(tick_count):
        micro_idx = jnp.clip(step_no - delay_by, 0, MICRO - 1)
        own_grad = lax.dynamic_index_in_dim(out_grad, micro_idx, 0, keepdims=False)
        grad_out = jnp.where(section_no == section_count - 1, own_grad, arrived_grad).astype(
            jnp.float32
        )
        grad_in, kept_rows, gain_grads = layer_backward(
            grad_out, back_mats, gain_pair, pick(tables_all, micro_idx), pick(stored_all, micro_idx)
        )
        sent_grad = grad_in.astype(jnp.bfloat16)
        grads_in.append(sent_grad)
        kept_list.append(kept_rows)
        gain_list.append(gain_grads)
        if step_no + 1 < tick_count:
            arrived_grad = passed_along(sent_grad, "section", -1)
    input_grad = lax.dynamic_slice_in_dim(jnp.stack(grads_in), delay_by, MICRO, 0)
    kept_all = stack_slice(kept_list, delay_by, MICRO)
    gain_total = jnp.sum(lax.dynamic_slice_in_dim(jnp.stack(gain_list), delay_by, MICRO, 0), 0)
    shares = None
    for index_m in range(MICRO):
        terms = weight_grads(pick(kept_all, index_m))
        term_query, term_key, term_value, term_out, term_gate, term_up, term_down = tuple(
            (term.reshape(owner_count, -1) for term in terms)
        )
        part_sums = (
            lax.psum_scatter(term_query, "dp", scatter_dimension=0, tiled=True),
            lax.psum_scatter(term_key, "dp", scatter_dimension=0, tiled=True),
            lax.psum_scatter(term_value, "dp", scatter_dimension=0, tiled=True),
            lax.psum_scatter(term_out, "dp", scatter_dimension=0, tiled=True),
            lax.psum_scatter(term_gate, "dp", scatter_dimension=0, tiled=True),
            lax.psum_scatter(term_up, "dp", scatter_dimension=0, tiled=True),
            lax.psum_scatter(term_down, "dp", scatter_dimension=0, tiled=True),
        )
        shares = part_sums if shares is None else jax.tree.map(jnp.add, shares, part_sums)
    gain_sum = lax.psum(gain_total, "dp")
    return (
        layer_out[None],
        input_grad[None],
        shares[0],
        shares[1],
        shares[2],
        shares[3],
        shares[4],
        shares[5],
        shares[6],
        gain_sum[0:1],
        gain_sum[1:2],
    )


def solution(mesh):
    placed = (
        P(None, "dp", None),
        P(None, "dp", None),
        P("section", "dp"),
        P("section", "dp"),
        P("section", "dp"),
        P("section", "dp"),
        P("section", "dp"),
        P("section", "dp"),
        P("section", "dp"),
        P("section", None),
        P("section", None),
        P(None, "dp", None),
    )
    return jax.shard_map(
        shards,
        mesh=mesh,
        in_specs=placed,
        out_specs=(
            P("section", None, "dp", None),
            P("section", None, "dp", None),
            P("section", "dp"),
            P("section", "dp"),
            P("section", "dp"),
            P("section", "dp"),
            P("section", "dp"),
            P("section", "dp"),
            P("section", "dp"),
            P("section", None),
            P("section", None),
        ),
        check_vma=False,
    )
```

profile of v0, /device:TPU:0, one launch (start us, length us, event | category | flops | bytes accessed | tf_op | source)
XLA Modules:
  0.0 690.1 jit_solution(4659663779009016096)
XLA Ops:
  13.5 25.0 %all-gather.1 = bf16[16,1,6912]{2,1,0:T(2,128)(2,1)S(1)} all-gather(bf16[1,1,6912]{2,1,0:T(2,128)(2,1)S(1)} %bitcast.950), channel_id=1, replica_groups=mesh['section'=2,'dp'=16] {'dp'}, dimensions={0}, use_global_device_ids=true | all-gather | bytes 235008 | tf_op jit(solution)/shard_map/all_gather | solution.py:328
  41.0 20.4 %all-gather = bf16[16,1,6912]{2,1,0:T(2,128)(2,1)S(1)} all-gather(bf16[1,1,6912]{2,1,0:T(2,128)(2,1)S(1)} %bitcast.951), channel_id=1, replica_groups=mesh['section'=2,'dp'=16] {'dp'}, dimensions={0}, use_global_device_ids=true | all-gather | bytes 235008 | tf_op jit(solution)/shard_map/all_gather | solution.py:329
  63.1 25.5 %all-gather.2 = bf16[16,1,20736]{2,1,0:T(2,128)(2,1)S(1)} all-gather(bf16[1,1,20736]{2,1,0:T(2,128)(2,1)S(1)} %bitcast.946), channel_id=1, replica_groups=mesh['section'=2,'dp'=16] {'dp'}, dimensions={0}, use_global_device_ids=true | all-gather | bytes 705024 | tf_op jit(solution)/shard_map/all_gather | solution.py:327
  88.6 4.0 reduce.3
  94.0 30.9 %all-gather.3 = bf16[16,1,20736]{2,1,0:T(2,128)(2,1)S(1)} all-gather(bf16[1,1,20736]{2,1,0:T(2,128)(2,1)} %bitcast.947), channel_id=1, replica_groups=mesh['section'=2,'dp'=16] {'dp'}, dimensions={0}, use_global_device_ids=true | all-gather | bytes 705024 | tf_op jit(solution)/shard_map/all_gather | solution.py:330
  124.8 4.9 reduce.4
  141.6 38.2 %reduce.6 = bf16[16,55296]{1,0:T(8,128)(2,1)S(1)} reduce(bf16[16,1,55296]{2,1,0:T(2,128)(2,1)} %all-gather.11.cloned.1.call-done, bf16[]{:T(256)} %constant.948), dimensions={1}, to_apply=%all-gather.4.reduce_sub_computation | reduce | bytes 3538946 | tf_op jit(solution)/shard_map/all_gather | solution.py:331
  182.6 39.1 %reduce.7 = bf16[16,55296]{1,0:T(8,128)(2,1)} reduce(bf16[16,1,55296]{2,1,0:T(2,128)(2,1)} %all-gather.13.cloned.1.call-done, bf16[]{:T(256)} %constant.948), dimensions={1}, to_apply=%all-gather.5.reduce_sub_computation | reduce | bytes 3538946 | tf_op jit(solution)/shard_map/all_gather | solution.py:332
  221.7 4.0 reshape.738
  225.8 39.0 %reduce.8 = bf16[16,55296]{1,0:T(8,128)(2,1)} reduce(bf16[16,1,55296]{2,1,0:T(2,128)(2,1)} %all-gather.15.cloned.1.call-done, bf16[]{:T(256)} %constant.948), dimensions={1}, to_apply=%all-gather.6.reduce_sub_computation | reduce | bytes 3538946 | tf_op jit(solution)/shard_map/all_gather | solution.py:333
  264.8 4.4 reshape.739
  275.4 3.9 collective-permute-start
  281.3 4.3 collective-permute-done
  294.9 4.9 collective-permute-start.1
  300.0 5.3 collective-permute-done.1
  334.8 6.3 collective-permute-done.2
  384.7 3.1 copy.85
  387.9 4.8 reshape.775
  395.0 3.0 reshape.773
  401.6 3.1 reshape.774
  412.8 32.9 %psum.7 = f32[2,576]{1,0:T(2,128)S(1)} all-reduce(f32[2,576]{1,0:T(2,128)} %fusion.265), channel_id=1, replica_groups=mesh['section'=2,'dp'=16] {'dp'}, use_global_device_ids=true, to_apply=%region_49.50 | all-reduce | flops 1152 | bytes 9216 | tf_op jit(solution)/shard_map/psum | solution.py:403
  449.0 216.0 %all-reduce.10.cloned.1.call-done = (f32[16,20736]{1,0:T(8,128)}, f32[16,6912]{1,0:T(8,128)}, f32[16,6912]{1,0:T(8,128)}, f32[16,20736]{1,0:T(8,128)}, f32[16,55...) async-done(((f32[16,20736]{1,0:T(8,128)}, f32[16,6912]{1,0:T(8,128)}, f32[16,6912]{1,0:T(8,128)}, f32[16,20736]{1,0:T(8,128)}, f32[16,55296]{1,0:T(8,128)}, ...) | async-done | bytes 14155792
  674.3 2.9 constant_dynamic-slice_fusion.20
  677.2 2.9 constant_dynamic-slice_fusion.19
  (498 shorter events, 144.6 us)
Async XLA Ops:
  7.2 134.4 %all-gather.11.cloned.1.call-start = ((), (), s32[]{:S(2)}) async-start(), calls=%async_computation | async-start | bytes 3760128 | tf_op jit(solution)/shard_map/all_gather | solution.py:331
  8.0 174.6 %all-gather.13.cloned.1.call-start = ((), (), s32[]{:S(2)}) async-start(), calls=%async_computation.1 | async-start | bytes 3760128 | tf_op jit(solution)/shard_map/all_gather | solution.py:332
  8.7 217.0 %all-gather.15.cloned.1.call-start = ((), (), s32[]{:S(2)}) async-start(), calls=%async_computation.2 | async-start | bytes 3760128 | tf_op jit(solution)/shard_map/all_gather | solution.py:333
  9.4 655.6 %all-reduce.10.cloned.1.call-start = ((), (), s32[]{:S(2)}) async-start(), calls=%async_computation.3 | async-start | bytes 28311552
  10.7 30.4 %copy-start.117 = (bf16[1,6912]{1,0:T(2,128)(2,1)S(1)}, bf16[1,6912]{1,0:T(2,128)(2,1)}, u32[]{:S(2)}) copy-start(bf16[1,6912]{1,0:T(2,128)(2,1)} %param.16) | copy-start | bytes 41476
  38.5 24.6 %copy-start.113 = (bf16[1,20736]{1,0:T(2,128)(2,1)S(1)}, bf16[1,20736]{1,0:T(2,128)(2,1)}, u32[]{:S(2)}) copy-start(bf16[1,20736]{1,0:T(2,128)(2,1)} %param.14) | copy-start | bytes 124420
  40.2 48.4 %copy-start.24 = (bf16[576,192]{1,0:T(8,128)(2,1)}, bf16[576,192]{1,0:T(8,128)(2,1)S(1)}, u32[]{:S(2)}) copy-start(bf16[576,192]{1,0:T(8,128)(2,1)S(1)} %reshape.734) | copy-start | bytes 663556
  63.1 72.8 %copy-start.21 = (bf16[576,192]{1,0:T(8,128)(2,1)}, bf16[576,192]{1,0:T(8,128)(2,1)S(1)}, u32[]{:S(2)}) copy-start(bf16[576,192]{1,0:T(8,128)(2,1)S(1)} %reshape.732) | copy-start | bytes 663556
  93.6 31.2 %copy-start.7 = (bf16[576,576]{1,0:T(8,128)(2,1)}, bf16[576,576]{1,0:T(8,128)(2,1)S(1)}, u32[]{:S(2)}) copy-start(bf16[576,576]{1,0:T(8,128)(2,1)S(1)} %reshape.735) | copy-start | bytes 1990660
  94.0 42.3 %copy-start.12 = (bf16[576,576]{1,0:T(8,128)(2,1)}, bf16[576,576]{1,0:T(8,128)(2,1)S(1)}, u32[]{:S(2)}) copy-start(bf16[576,576]{1,0:T(8,128)(2,1)S(1)} %copy.70) | copy-start | bytes 1990660
  131.9 7.5 %copy-start.5 = (bf16[576,576]{1,0:T(8,128)(2,1)}, bf16[576,576]{1,0:T(8,128)(2,1)S(1)}, u32[]{:S(2)}) copy-start(bf16[576,576]{1,0:T(8,128)(2,1)S(1)} %reshape.736) | copy-start | bytes 1990660
  275.4 10.2 %collective-permute-start = (bf16[256,576]{0,1:T(8,128)(2,1)}, bf16[256,576]{0,1:T(8,128)(2,1)}, u32[]{:S(2)}, u32[]{:S(2)}) collective-permute-start(bf16[256,576]{0,1:T(8,128)(2,1)} %fusion.54), channel_id=1, source_target_pairs={{0,16},{1,17},{2,18},{3,19},{4,20},{5,21},{6,22},{7,23},{8,24},{9,... | collective-permute-start | bytes 884744 | tf_op jit(solution)/shard_map/ppermute | solution.py:25
  294.0 11.3 %copy-start.36 = (bf16[2,256,576]{1,2,0:T(8,128)(2,1)S(1)}, bf16[2,256,576]{1,2,0:T(8,128)(2,1)}, u32[]{:S(2)}) copy-start(bf16[2,256,576]{1,2,0:T(8,128)(2,1)} %param.12) | copy-start | bytes 1769476
  294.9 10.4 %collective-permute-start.1 = (bf16[256,576]{0,1:T(8,128)(2,1)S(1)}, bf16[256,576]{0,1:T(8,128)(2,1)S(1)}, u32[]{:S(2)}, u32[]{:S(2)}) collective-permute-start(bf16[256,576]{0,1:T(8,128)(2,1)S(1)} %fusion.55), channel_id=1, source_target_pairs={{0,16},{1,17},{2,18},{3,19},{4,20},{5,21},{6,22},{7,23},{8,24},{9,... | collective-permute-start | bytes 884744 | tf_op jit(solution)/shard_map/ppermute | solution.py:25
  311.4 40.1 %copy-start.3 = (f32[3,256,576]{1,2,0:T(8,128)}, f32[3,256,576]{1,2,0:T(8,128)S(1)}, u32[]{:S(2)}) copy-start(f32[3,256,576]{1,2,0:T(8,128)S(1)} %pad_maximum_fusion.4) | copy-start | bytes 5308420
  315.3 19.1 %copy-start.37 = (bf16[256,1536]{1,0:T(8,128)(2,1)}, bf16[256,1536]{1,0:T(8,128)(2,1)S(1)}, u32[]{:S(2)}) copy-start(bf16[256,1536]{1,0:T(8,128)(2,1)S(1)} %get-tuple-element.315) | copy-start | bytes 2359300
  322.2 22.8 %copy-start.61 = (bf16[3,256,3,64]{1,3,2,0:T(8,128)(2,1)}, bf16[3,256,3,64]{1,3,2,0:T(8,128)(2,1)S(1)}, u32[]{:S(2)}) copy-start(bf16[3,256,3,64]{1,3,2,0:T(8,128)(2,1)S(1)} %pad_maximum_fusion.13) | copy-start | bytes 884740
  322.8 24.8 %copy-start.50 = (bf16[3,256,3,64]{1,3,2,0:T(8,128)(2,1)}, bf16[3,256,3,64]{1,3,2,0:T(8,128)(2,1)S(1)}, u32[]{:S(2)}) copy-start(bf16[3,256,3,64]{1,3,2,0:T(8,128)(2,1)S(1)} %pad_maximum_fusion.12) | copy-start | bytes 884740
  323.4 24.6 %copy-start.17 = (bf16[3,256,3,3,64]{1,4,3,2,0:T(8,128)(2,1)}, bf16[3,256,3,3,64]{1,4,3,2,0:T(8,128)(2,1)S(1)}, u32[]{:S(2)}) copy-start(bf16[3,256,3,3,64]{1,4,3,2,0:T(8,128)(2,1)S(1)} %pad_maximum_fusion.5) | copy-start | bytes 2654212
  331.4 9.7 %collective-permute-start.2 = (bf16[256,576]{0,1:T(8,128)(2,1)S(1)}, bf16[256,576]{0,1:T(8,128)(2,1)S(1)}, u32[]{:S(2)}, u32[]{:S(2)}) collective-permute-start(bf16[256,576]{0,1:T(8,128)(2,1)S(1)} %get-tuple-element.286), channel_id=1, source_target_pairs={{16,0},{17,1},{18,2},{19,3},{20,4},{21,5},{22,6},{23,7},{24,8},{25... | collective-permute-start | bytes 884744 | tf_op jit(solution)/shard_map/ppermute | solution.py:25
  351.8 8.6 %collective-permute-start.3 = (bf16[256,576]{0,1:T(8,128)(2,1)S(1)}, bf16[256,576]{0,1:T(8,128)(2,1)S(1)}, u32[]{:S(2)}, u32[]{:S(2)}) collective-permute-start(bf16[256,576]{0,1:T(8,128)(2,1)S(1)} %fusion.141), channel_id=1, source_target_pairs={{16,0},{17,1},{18,2},{19,3},{20,4},{21,5},{22,6},{23,7},{24,8},{25... | collective-permute-start | bytes 884744 | tf_op jit(solution)/shard_map/ppermute | solution.py:25
  410.7 35.7 %copy-start.34 = (f32[256,576]{0,1:T(8,128)S(1)}, f32[256,576]{0,1:T(8,128)}, u32[]{:S(2)}) copy-start(f32[256,576]{0,1:T(8,128)} %copy-done.33) | copy-start | bytes 1769476
  411.3 36.0 %copy-start.65 = (bf16[256,576]{0,1:T(8,128)(2,1)S(1)}, bf16[256,576]{0,1:T(8,128)(2,1)}, u32[]{:S(2)}) copy-start(bf16[256,576]{0,1:T(8,128)(2,1)} %copy-done.64) | copy-start | bytes 884740
  411.3 36.0 %copy-start.67 = (bf16[256,576]{0,1:T(8,128)(2,1)S(1)}, bf16[256,576]{0,1:T(8,128)(2,1)}, u32[]{:S(2)}) copy-start(bf16[256,576]{0,1:T(8,128)(2,1)} %copy-done.66) | copy-start | bytes 884740
  (111 other events, 242.8 us)
Sparse Core Ops, SparseCore 0:
  10.3 53.8 all-gather.10
  66.5 55.0 all-gather.12
  124.0 50.9 all-gather.14
  404.9 260.1 all-reduce.9
where the time goes:
time: 700 us; the launch traced here: 690 us
  waiting for transfers between devices  236 us (34%)
  other arithmetic  165 us (24%)
  blocking collectives  135 us (19%)
  local copies, waits for them, and re-layouts  74.7 us (11%)
  matrix products  51.4 us (7%)
  between operations  16.4 us (2%)
  starting transfers between devices  11.9 us (2%)
    unnamed x5, waiting for transfers between devices  218 us
    all_gather x1, other arithmetic, shards(): lax.all_gather(w_up, 'dp', axis=0, tiled=True)  39.1 us
    all_gather x1, other arithmetic, shards(): lax.all_gather(w_down, 'dp', axis=0, tiled=True)  39 us
    all_gather x1, other arithmetic, shards(): lax.all_gather(w_gate, 'dp', axis=0, tiled=True)  38.2 us
    unnamed x263, local copies, waits for them, and re-layouts  34.9 us
    psum x1, blocking collectives, shards(): gain_sum = lax.psum(gain_total, 'dp')  32.9 us
    all_gather x1, blocking collectives, shards(): lax.all_gather(w_out, 'dp', axis=0, tiled=True)  30.9 us
    all_gather x1, blocking collectives, shards(): lax.all_gather(w_query, 'dp', axis=0, tiled=True)  25.5 us
  transfers between devices with their start and end apart: 8, of which 5 were waited for; matrix products, arithmetic and copies ran while one was open for 19% of the time, Pallas kernels for 0%

commit v1 on v0

v1 whole, which is shorter than its diff:
```python
import functools
import math

import jax
import jax.numpy as jnp
from jax import lax
from jax.experimental import pallas as pl
from jax.experimental.pallas import tpu as pltpu
from jax.sharding import PartitionSpec as P

D = 576
HEADS = 9
KV_HEADS = 3
HEAD = 64
FF = 1536
TOK_MB = 256
QW = HEADS * HEAD
KVW = KV_HEADS * HEAD
REP = HEADS // KV_HEADS

EPS = 1e-05
THETA = 100000.0
NEG = -1000000000.0

PAD = 640
COL_K = QW
COL_O = QW + KVW
COL_V = COL_O + D
COL_VX = 1280
SKIP_V = COL_V - COL_VX

BF = jnp.bfloat16
F32 = jnp.float32

PARAMS = pltpu.CompilerParams(vmem_limit_bytes=50 * 1024 * 1024)


def dot(left, right):
    return lax.dot_general(left, right, (((1,), (0,)), ((), ())), preferred_element_type=F32)


def dot_nt(left, right):
    return lax.dot_general(left, right, (((1,), (1,)), ((), ())), preferred_element_type=F32)


def dot_tn(left, right):
    return lax.dot_general(left, right, (((0,), (0,)), ((), ())), preferred_element_type=F32)


def spread(rows, place):
    return dot(rows, place).astype(BF)


def collect(rows, place):
    high = rows.astype(BF)
    low = (rows - high.astype(F32)).astype(BF)
    return dot_nt(high, place) + dot_nt(low, place)


def turned(tile):
    lane = lax.broadcasted_iota(jnp.int32, tile.shape, 1)
    return jnp.where(lane % HEAD < HEAD // 2, pltpu.roll(tile, 128 - HEAD // 2, 1), pltpu.roll(tile, HEAD // 2, 1))


def inv_rms(stream):
    return lax.rsqrt(jnp.mean(stream * stream, -1, keepdims=True) + EPS)


def norm_back(stream, gain_row, grad_normed):
    scale_r = inv_rms(stream)
    weighted = grad_normed * gain_row
    grad_stream = scale_r * weighted - stream * scale_r**3 * jnp.mean(
        stream * weighted, -1, keepdims=True
    )
    grad_gain = jnp.sum(grad_normed * stream * scale_r, 0, keepdims=True)
    return (grad_stream, grad_gain)


CHUNK = 512


def forward_kernel(save, x_ref, att_ref, gate_ref, up_ref, down_ref, ga_ref, gb_ref, place_ref, cos_ref, sin_ref, mask_ref, out_ref, *saved):
    if save:
        na_ref, qk_ref, v_ref, lse_ref, mx_ref, mid_ref, nb_ref, g_ref, u_ref, act_ref = saved
    place = place_ref[...]
    stream = x_ref[...].astype(F32)
    normed_a = spread((stream * inv_rms(stream) * ga_ref[...]).astype(BF), place)
    raw = dot(normed_a, att_ref[:, :COL_O])
    cosine, sine = cos_ref[...], sin_ref[...]
    tiles = []
    for j in range(COL_O // 128):
        tile = raw[:, 128 * j : 128 * (j + 1)]
        tiles.append((tile * cosine + turned(tile) * sine).astype(BF))
    qk = jnp.concatenate(tiles, 1)
    value = dot(normed_a, att_ref[:, COL_VX:])[:, SKIP_V:].astype(BF)
    allowed = mask_ref[...] > 0.5
    mixed = []
    for h in range(HEADS):
        kv = h // REP
        query = qk[:, HEAD * h : HEAD * (h + 1)]
        key = qk[:, COL_K + HEAD * kv : COL_K + HEAD * (kv + 1)]
        scores = jnp.where(allowed, dot_nt(query, key) * HEAD ** (-0.5), NEG)
        row_max = jnp.max(scores, -1, keepdims=True)
        terms = jnp.exp(scores - row_max)
        total = jnp.sum(terms, -1, keepdims=True)
        attend = (terms * (1.0 / total)).astype(BF)
        mixed.append(dot(attend, value[:, HEAD * kv : HEAD * (kv + 1)]).astype(BF))
        if save:
            lse_ref[:, h : h + 1] = row_max + jnp.log(total)
    mixed_p = spread(jnp.concatenate(mixed, 1), place)
    middle = stream + dot(mixed_p, att_ref[:, COL_O : COL_O + D])
    normed_b = spread((middle * inv_rms(middle) * gb_ref[...]).astype(BF), place)
    result = middle
    for c in range(0, FF, CHUNK):
        gate = dot(normed_b, gate_ref[:, c : c + CHUNK])
        up = dot(normed_b, up_ref[:, c : c + CHUNK])
        act = (gate * jax.nn.sigmoid(gate) * up).astype(BF)
        result = result + dot(act, down_ref[c : c + CHUNK, :])
        if save:
            g_ref[:, c : c + CHUNK] = gate
            u_ref[:, c : c + CHUNK] = up
            act_ref[:, c : c + CHUNK] = act
    out_ref[...] = result.astype(BF)
    if save:
        na_ref[...] = normed_a
        qk_ref[...] = qk
        v_ref[...] = value
        mx_ref[...] = mixed_p
        mid_ref[...] = middle
        nb_ref[...] = normed_b


def backward_kernel(save, grad_ref, x_ref, att_ref, gate_ref, up_ref, down_ref, ga_ref, gb_ref, place_ref, cos_ref, sin_ref, mask_ref,
                    qk_ref, v_ref, lse_ref, mid_ref, g_ref, u_ref, in_ref, *kept):
    if save:
        dqk_ref, dv_ref, gattn_ref, dg_ref, du_ref, gains_ref = kept
    place = place_ref[...]
    grad_low = grad_ref[...]
    grad_out = grad_low.astype(F32)
    back_p = jnp.zeros((TOK_MB, PAD), F32)
    for c in range(0, FF, CHUNK):
        grad_act = dot_nt(grad_low, down_ref[c : c + CHUNK, :])
        gate = g_ref[:, c : c + CHUNK]
        up = u_ref[:, c : c + CHUNK]
        sig = jax.nn.sigmoid(gate)
        acts = grad_act * sig
        d_gate = (acts * up * (1.0 + gate * (1.0 - sig))).astype(BF)
        d_up = (acts * gate).astype(BF)
        back_p = back_p + dot_nt(d_gate, gate_ref[:, c : c + CHUNK]) + dot_nt(d_up, up_ref[:, c : c + CHUNK])
        if save:
            dg_ref[:, c : c + CHUNK] = d_gate
            du_ref[:, c : c + CHUNK] = d_up
    back_b, gain_b = norm_back(mid_ref[...], gb_ref[...], collect(back_p, place))
    grad_middle = grad_out + back_b
    grad_attn = grad_middle.astype(BF)
    grad_mixed = dot_nt(dot_nt(grad_attn, att_ref[:, COL_O : COL_O + D]).astype(BF), place).astype(BF)
    allowed = mask_ref[...] > 0.5
    d_query, d_key, d_value = [], [], []
    for kv in range(KV_HEADS):
        key = qk_ref[:, COL_K + HEAD * kv : COL_K + HEAD * (kv + 1)]
        value = v_ref[:, HEAD * kv : HEAD * (kv + 1)]
        sum_k, sum_v = None, None
        for h in range(kv * REP, (kv + 1) * REP):
            query = qk_ref[:, HEAD * h : HEAD * (h + 1)]
            grad_h = grad_mixed[:, HEAD * h : HEAD * (h + 1)]
            scores = jnp.where(allowed, dot_nt(query, key) * HEAD ** (-0.5), NEG)
            attend = jnp.exp(scores - lse_ref[:, h : h + 1])
            grad_attend = dot_nt(grad_h, value)
            inner = jnp.sum(attend * grad_attend, -1, keepdims=True)
            grad_scores = (attend * (grad_attend - inner)).astype(BF)
            part_v = dot_tn(attend.astype(BF), grad_h)
            part_k = dot_tn(grad_scores, query)
            sum_v = part_v if sum_v is None else sum_v + part_v
            sum_k = part_k if sum_k is None else sum_k + part_k
            d_query.append(dot(grad_scores, key) * HEAD ** (-0.5))
        d_key.append(sum_k * HEAD ** (-0.5))
        d_value.append(sum_v.astype(BF))
    raw = jnp.concatenate(d_query + d_key, 1)
    cosine, sine = cos_ref[...], sin_ref[...]
    tiles = []
    for j in range(COL_O // 128):
        tile = raw[:, 128 * j : 128 * (j + 1)]
        tiles.append((tile * cosine - turned(tile) * sine).astype(BF))
    d_qk = jnp.concatenate(tiles, 1)
    d_v = jnp.concatenate([jnp.zeros((TOK_MB, SKIP_V), BF)] + d_value, 1)
    back_p = dot_nt(d_qk, att_ref[:, :COL_O]) + dot_nt(d_v, att_ref[:, COL_VX:])
    back_a, gain_a = norm_back(x_ref[...].astype(F32), ga_ref[...], collect(back_p, place))
    in_ref[...] = (grad_middle + back_a).astype(BF)
    if save:
        dqk_ref[...] = d_qk
        dv_ref[...] = d_v
        gattn_ref[...] = grad_attn
        gains_ref[0:1, :] = gain_a
        gains_ref[1:2, :] = gain_b


def weights_kernel(*refs):
    ins, (att_out, gate_out, up_out, down_out) = refs[:-4], refs[-4:]
    half = len(ins) // 2
    pairs = [jnp.concatenate([one[...], two[...]], 0) for one, two in zip(ins[:half], ins[half:])]
    normed_a, mixed, normed_b, act, d_qk, d_v, grad_attn, d_gate, d_up, grad_down = pairs
    att_out[:, :COL_O] = dot_tn(normed_a, d_qk).astype(BF)
    att_out[:, COL_O:COL_VX] = dot_tn(mixed, grad_attn[:, : COL_VX - COL_O]).astype(BF)
    grad_v = dot_tn(normed_a, d_v)
    grad_o = dot_tn(mixed, grad_attn[:, COL_VX - COL_O :])
    grad_o = jnp.concatenate([grad_o, jnp.zeros((PAD, KVW), F32)], 1)
    att_out[:, COL_VX:] = (grad_v + grad_o).astype(BF)
    for c in range(0, FF, CHUNK):
        gate_out[:, c : c + CHUNK] = dot_tn(normed_b, d_gate[:, c : c + CHUNK]).astype(BF)
        up_out[:, c : c + CHUNK] = dot_tn(normed_b, d_up[:, c : c + CHUNK]).astype(BF)
        down_out[c : c + CHUNK, :] = dot_tn(act[:, c : c + CHUNK], grad_down).astype(BF)


def shape(*dims, dtype=BF):
    return jax.ShapeDtypeStruct(dims, dtype)


def run_forward(save, *operands):
    outs = [shape(TOK_MB, D)]
    if save:
        outs += [
            shape(TOK_MB, PAD),
            shape(TOK_MB, COL_O),
            shape(TOK_MB, KVW),
            shape(TOK_MB, 128, dtype=F32),
            shape(TOK_MB, PAD),
            shape(TOK_MB, D, dtype=F32),
            shape(TOK_MB, PAD),
            shape(TOK_MB, FF, dtype=F32),
            shape(TOK_MB, FF, dtype=F32),
            shape(TOK_MB, FF),
        ]
    return pl.pallas_call(
        functools.partial(forward_kernel, save), out_shape=outs, compiler_params=PARAMS, name="layer_forward"
    )(*operands)


def run_backward(save, *operands):
    outs = [shape(TOK_MB, D)]
    if save:
        outs += [
            shape(TOK_MB, COL_O),
            shape(TOK_MB, QW + D + 2 * KVW - COL_VX),
            shape(TOK_MB, D),
            shape(TOK_MB, FF),
            shape(TOK_MB, FF),
            shape(2, D, dtype=F32),
        ]
    return pl.pallas_call(
        functools.partial(backward_kernel, save), out_shape=outs, compiler_params=PARAMS, name="layer_backward"
    )(*operands)


def make_tables(seg_row):
    count_t = seg_row.shape[0]
    order_idx = jnp.arange(count_t, dtype=jnp.int32)
    same_doc = seg_row[:, None] == seg_row[None, :]
    before = order_idx[None, :] < order_idx[:, None]
    positions = jnp.sum(jnp.where(same_doc & before, jnp.float32(1.0), jnp.float32(0.0)), axis=1)
    allowed = same_doc & (order_idx[None, :] <= order_idx[:, None])
    inv_freq = jnp.exp(jnp.arange(HEAD // 2, dtype=jnp.float32) * (-2.0 * math.log(THETA) / HEAD))
    angles = positions[:, None] * inv_freq[None, :]
    cosine, sine = jnp.cos(angles), jnp.sin(angles)
    cosine = jnp.concatenate([cosine] * 4, -1)
    sine = jnp.concatenate([-sine, sine] * 2, -1)
    return (cosine, sine, allowed.astype(F32))


def placement(rows_each, rows_padded):
    row = lax.broadcasted_iota(jnp.int32, (D, PAD), 0)
    col = lax.broadcasted_iota(jnp.int32, (D, PAD), 1)
    return (col == row + (row // rows_each) * (rows_padded - rows_each)).astype(BF)


def gather_weights(shard, owners):
    w_query, w_key, w_value, w_out, w_gate, w_up, w_down = shard
    if D % owners == 0 and PAD % owners == 0 and FF % owners == 0:
        rows, padded = D // owners, PAD // owners
        att = jnp.concatenate(
            [w_query.reshape(rows, QW), w_key.reshape(rows, KVW), w_out.reshape(rows, D), w_value.reshape(rows, KVW)], 1
        )
        parts = [att, w_gate.reshape(rows, FF), w_up.reshape(rows, FF), w_down.reshape(rows, FF)]
        packed = jnp.concatenate([jnp.pad(part, ((0, padded - rows), (0, 0))) for part in parts], 0)
        whole = lax.all_gather(packed, "dp", axis=0, tiled=True).reshape(owners, 4, padded, FF)
        att, gate, up = (whole[:, i].reshape(PAD, FF) for i in range(3))
        down = whole[:, 3, :rows].reshape(FF, D)
        return att, gate, up, down, placement(rows, padded)
    w_query, w_key, w_value, w_out, w_gate, w_up, w_down = (
        lax.all_gather(member, "dp", axis=0, tiled=True) for member in (w_query[0], w_key[0], w_value[0], w_out[0], w_gate[0], w_up[0], w_down[0])
    )
    att = jnp.concatenate(
        [w_query.reshape(D, QW), w_key.reshape(D, KVW), w_out.reshape(QW, D), w_value.reshape(D, KVW)], 1
    )
    att, gate, up = (jnp.pad(m, ((0, PAD - D), (0, 0))) for m in (att, w_gate.reshape(D, FF), w_up.reshape(D, FF)))
    return att, gate, up, w_down.reshape(FF, D), placement(D, D)


def cut(att):
    return att[:, :QW], att[:, COL_K:COL_O], att[:, COL_V:], att[:, COL_O:COL_V]


def scatter_grads(grads, owners):
    att, gate, up, down = grads
    if D % owners == 0 and PAD % owners == 0 and FF % owners == 0:
        rows, padded = D // owners, PAD // owners
        down = jnp.pad(down.reshape(owners, rows, FF), ((0, 0), (0, padded - rows), (0, 0)))
        packed = jnp.stack([att.reshape(owners, padded, FF), gate.reshape(owners, padded, FF), up.reshape(owners, padded, FF), down], 1)
        packed = packed.reshape(owners * 4 * padded, FF)
        share = lax.psum_scatter(packed, "dp", scatter_dimension=0, tiled=True)
        share = share.reshape(4, padded, FF)[:, :rows].astype(F32)
        pieces = cut(share[0]) + (share[1], share[2], share[3])
        return tuple(piece.reshape(1, -1) for piece in pieces)
    pieces = cut(att[:D]) + (gate[:D], up[:D], down)
    return tuple(
        lax.psum_scatter(piece.reshape(owners, -1), "dp", scatter_dimension=0, tiled=True).astype(F32) for piece in pieces
    )


def shards(
    tokens,
    segments,
    w_query,
    w_key,
    w_value,
    w_out,
    w_gate,
    w_up,
    w_down,
    attn_gain,
    mlp_gain,
    out_grad,
):
    first = lax.axis_index("section") == 0
    owners = lax.axis_size("dp")
    *mats, place = gather_weights((w_query, w_key, w_value, w_out, w_gate, w_up, w_down), owners)
    tables = jax.vmap(make_tables)(segments[:, 0])

    def tables_of(own):
        return tuple(lax.dynamic_index_in_dim(t, own, 0, keepdims=False) for t in tables)

    def send_on(block):
        return lax.ppermute(block, "section", [(0, 1)])

    def send_back(block):
        return lax.ppermute(block, "section", [(1, 0)])

    common = (*mats, attn_gain, mlp_gain, place)
    one, two = tables_of(0), tables_of(jnp.where(first, 1, 0))
    four = tables_of(jnp.where(first, 0, 1))
    sent = run_forward(False, tokens[0], *common, *one)[0]
    x_two = jnp.where(first, tokens[1], send_on(sent))
    out_two, *stored_two = run_forward(True, x_two, *common, *two)
    arrived = send_on(out_two)

    def back(save, grad, x_rows, tables_at, stored):
        normed_a, qk, value, lse, mixed, middle, normed_b, gate, up, act = stored
        return run_backward(save, grad, x_rows, *common, *tables_at, qk, value, lse, middle, gate, up)

    grad_three = back(False, out_grad[0], x_two, two, stored_two)[0]
    arrived_grad = send_back(grad_three)
    x_four = jnp.where(first, tokens[0], arrived)
    out_four, *stored_four = run_forward(True, x_four, *common, *four)
    grad_at_five = jnp.where(first, arrived_grad, out_grad[1])
    in_five, *kept_five = back(True, grad_at_five, x_four, four, stored_four)
    grad_at_six = jnp.where(first, send_back(in_five), out_grad[0])
    in_six, *kept_six = back(True, grad_at_six, x_two, two, stored_two)

    def rows_of(stored, kept, grad):
        normed_a, qk, value, lse, mixed, middle, normed_b, gate, up, act = stored
        d_qk, d_v, grad_attn, d_gate, d_up, gains = kept
        return (normed_a, mixed, normed_b, act, d_qk, d_v, grad_attn, d_gate, d_up, grad)

    grads = pl.pallas_call(
        weights_kernel,
        out_shape=[shape(PAD, FF), shape(PAD, FF), shape(PAD, FF), shape(FF, D)],
        compiler_params=PARAMS,
        name="weight_grads",
    )(*rows_of(stored_four, kept_five, grad_at_five), *rows_of(stored_two, kept_six, grad_at_six))
    gain_sum = lax.psum(kept_five[-1] + kept_six[-1], "dp")
    shares = scatter_grads(grads, owners)
    layer_out = jnp.stack([jnp.where(first, out_four, out_two), jnp.where(first, out_two, out_four)])
    input_grad = jnp.stack([jnp.where(first, in_five, in_six), jnp.where(first, in_six, in_five)])
    return (layer_out[None], input_grad[None], *shares, gain_sum[0:1], gain_sum[1:2])


def solution(mesh):
    weights = (P("section", "dp"),) * 7
    gains = (P("section", None),) * 2
    rows = P("section", None, "dp", None)
    return jax.shard_map(
        shards,
        mesh=mesh,
        in_specs=(P(None, "dp", None), P(None, "dp", None), *weights, *gains, P(None, "dp", None)),
        out_specs=(rows, rows, *weights, *gains),
        check_vma=False,
    )
```

time: 700 us -> 375 us (0.54)
  other arithmetic: 165 us -> 20.7 us
  blocking collectives: 135 us -> 30.2 us
  waiting for transfers between devices: 236 us -> 143 us
  Pallas kernels: 0 us -> 87.2 us
  matrix products: 51.4 us -> 0 us
  local copies, waits for them, and re-layouts: 74.7 us -> 62.1 us
    unnamed x5 -> x2, waiting for transfers between devices: 218 us -> 0.03 us
    all_gather x7 -> x0, other arithmetic: 128 us -> none  [the longest x1 39.1 us: shards(): lax.all_gather(w_up, 'dp', axis=0, tiled=True)]
    all_gather x4 -> x0, blocking collectives: 102 us -> none  [the longest x1 30.9 us: shards(): lax.all_gather(w_out, 'dp', axis=0, tiled=True)]
    pallas_call x0 -> x7, Pallas kernels: none -> 87.2 us  [the longest x3 43.2 us: run_backward(): pl.pallas_call(functools.partial(backward_kernel, save), out_shape=outs,...]
    all_gather x3 -> x1, waiting for transfers between devices: 0.04 us -> 68.1 us  [gather_weights(): lax.all_gather(packed, 'dp', axis=0, tiled=True)]
    reduce_scatter x0 -> x1, waiting for transfers between devices: none -> 58.8 us  [scatter_grads(): share = lax.psum_scatter(packed, 'dp', scatter_dimension=0, tiled=True)]
    dot_general x77 -> x0, matrix products: 51.4 us -> none  [the longest x21 17.1 us: matmul(): return jnp.dot(left, right, preferred_element_type=jnp.float32)]
    add x10 -> x0, local copies, waits for them, and re-layouts: 20.4 us -> none  [shards(): jax.tree.map(jnp.add, shares, part_sums)]
  transfers between devices with their start and end apart: 8 -> 6, of which waited for: 5 -> 4; matrix products, arithmetic and copies ran while one was open for 19% -> 4% of each run, Pallas kernels for 0% -> 7%
where the time goes in v1:
time: 375 us; the launch traced here: 371 us
  waiting for transfers between devices  143 us (38%)
  Pallas kernels  87.2 us (23%)
  local copies, waits for them, and re-layouts  62.1 us (17%)
  blocking collectives  30.2 us (8%)
  other arithmetic  20.7 us (6%)
  between operations  14.8 us (4%)
  starting transfers between devices  12.5 us (3%)
    all_gather x1, waiting for transfers between devices, gather_weights(): lax.all_gather(packed, 'dp', axis=0, tiled=True)  68.1 us
    reduce_scatter x1, waiting for transfers between devices, scatter_grads(): share = lax.psum_scatter(packed, 'dp', scatter_dimension=0, tiled=True)  58.8 us
    pallas_call x3, Pallas kernels, run_backward(): pl.pallas_call(functools.partial(backward_kernel, save), out_shape=outs,...  43.2 us
    pallas_call x3, Pallas kernels, run_forward(): pl.pallas_call(functools.partial(forward_kernel, save), out_shape=outs, c...  34.1 us
    psum x1, blocking collectives, shards(): gain_sum = lax.psum(kept_five[-1] + kept_six[-1], 'dp')  30.2 us
    unnamed x99, local copies, waits for them, and re-layouts  25.4 us
    ppermute x2, waiting for transfers between devices, send_back(): return lax.ppermute(block, 'section', [(1, 0)])  10.1 us
    pallas_call x1, Pallas kernels, shards(): pl.pallas_call(weights_kernel, out_shape=[shape(PAD, FF), shape(PAD, FF),...  9.91 us
  transfers between devices with their start and end apart: 6, of which 4 were waited for; matrix products, arithmetic and copies ran while one was open for 4% of the time, Pallas kernels for 7%

profile of v1, /device:TPU:0, one launch (start us, length us, event | category | flops | bytes accessed | tf_op | source)
XLA Modules:
  0.0 370.7 jit_solution(11578194303179812407)
XLA Ops:
  13.3 1.5 reduce.5
  15.0 1.5 reduce.6
  24.0 68.1 %all-gather.2.cloned.1.call-done = bf16[2560,1536]{1,0:T(8,128)(2,1)} async-done(((bf16[160,1536]{1,0:T(8,128)(2,1)}), bf16[2560,1536]{1,0:T(8,128)(2,1)}) %all-gather.2.cloned.1.call-update) | async-done | bytes 7864336 | tf_op jit(solution)/shard_map/all_gather | solution.py:284
  92.1 3.0 slice.84
  95.1 5.1 %fusion.15 = (bf16[16,1,40,1536]{3,2,1,0:T(8,128)(2,1)}, bf16[16,1,40,1536]{3,2,1,0:T(8,128)(2,1)}, bf16[16,1,40,1536]{3,2,1,0:T(8,128)(2,1)S(1)}) fusion(bf16[16,4,40,1536]{3,2,1,0:T(8,128)(2,1)} %bitcast.85), kind=kLoop, calls=%fused_computation.63 | loop fusion | bytes 11796480 | tf_op jit(solution)/shard_map/slice | solution.py:285
  100.2 5.7 %reshape_squeeze.24.down_ref = bf16[1536,576]{1,0:T(8,128)(2,1)} reshape(bf16[16,1,36,1536]{3,2,1,0:T(8,128)(2,1)} %slice.84) | data formatting | bytes 3538944 | tf_op jit(solution)/shard_map/reshape;squeeze | solution.py:286
  110.1 10.3 %layer_forward.3 = bf16[256,576]{1,0:T(8,128)(2,1)} custom-call(bf16[256,576]{1,0:T(8,128)(2,1)S(1)} %bitcast.69, bf16[640,1536]{1,0:T(8,128)(2,1)S(1)} %bitcast.63, bf16[640,1536]{1,0:T(8,128)(2,1)} %bitcast.77, bf16[640,1536]{1,0:T(8,128)(2,1)} %bitcast.71, bf16[1536,576]{1,0:T(8,128)(2,1)} %reshape_squeeze.24.down_ref, f32[1,576]{1,0:T(1,128)S(1)} %copy-done.31, ...), custom_call_target="tpu_custom_call" | custom-call | tf_op jit(solution)/shard_map/layer_forward/pallas_call | solution.py:233
  120.3 3.6 collective-permute-start
  125.1 6.3 %collective-permute-done = bf16[256,576]{1,0:T(8,128)(2,1)S(1)} collective-permute-done((bf16[256,576]{1,0:T(8,128)(2,1)}, bf16[256,576]{1,0:T(8,128)(2,1)S(1)}, u32[]{:S(2)}, u32[]{:S(2)}) %collective-permute-start) | collective-permute-done | bytes 294944 | tf_op jit(solution)/shard_map/ppermute | solution.py:342
  134.6 12.1 %layer_forward.4 = (bf16[256,576]{1,0:T(8,128)(2,1)}, bf16[256,640]{1,0:T(8,128)(2,1)S(1)}, bf16[256,768]{1,0:T(8,128)(2,1)S(1)}, bf16[256,192]{1,0:T(8,128)(2,1...) custom-call(bf16[256,576]{1,0:T(8,128)(2,1)S(1)} %bitcast_select_fus, ...), custom_call_target="tpu_custom_call" | custom-call | tf_op jit(solution)/shard_map/layer_forward/pallas_call | solution.py:233
  148.2 5.3 %collective-permute-start.1 = (bf16[256,576]{1,0:T(8,128)(2,1)}, bf16[256,576]{1,0:T(8,128)(2,1)}, u32[]{:S(2)}, u32[]{:S(2)}) collective-permute-start(bf16[256,576]{1,0:T(8,128)(2,1)} %get-tuple-element.51), channel_id=1, source_target_pairs={{0,16},{1,17},{2,18},{3,19},{4,20},{5,21},{6,22},{7,23},{8,24},{9,... | collective-permute-start | bytes 884744 | tf_op jit(solution)/shard_map/ppermute | solution.py:342
  158.8 14.6 %layer_backward.3 = bf16[256,576]{1,0:T(8,128)(2,1)} custom-call(bf16[256,576]{1,0:T(8,128)(2,1)S(1)} %bitcast.70, bf16[256,576]{1,0:T(8,128)(2,1)S(1)} %bitcast_select_fusion.1.x_ref, bf16[640,1536]{1,0:T(8,128)(2,1)} %bitcast.65, bf16[640,1536]{1,0:T(8,128)(2,1)} %bitcast.79, bf16[640,1536]{1,0:T(8,128)(2,1)} %bitcast.73, ...), custom_call_target="tpu_custom_call" | custom-call | tf_op jit(solution)/shard_map/layer_backward/pallas_call | solution.py:249
  173.4 1.7 collective-permute-start.2
  179.5 11.7 %layer_forward.5 = (bf16[256,576]{1,0:T(8,128)(2,1)S(1)}, bf16[256,640]{1,0:T(8,128)(2,1)S(1)}, bf16[256,768]{1,0:T(8,128)(2,1)S(1)}, bf16[256,192]{1,0:T(8,128)...) custom-call(bf16[256,576]{1,0:T(8,128)(2,1)S(1)} %broadcast_select_f, ...), custom_call_target="tpu_custom_call" | custom-call | tf_op jit(solution)/shard_map/layer_forward/pallas_call | solution.py:233
  192.3 14.4 %layer_backward.4 = (bf16[256,576]{1,0:T(8,128)(2,1)S(1)}, bf16[256,768]{1,0:T(8,128)(2,1)S(1)}, bf16[256,256]{1,0:T(8,128)(2,1)S(1)}, bf16[256,576]{1,0:T(8,128...) custom-call(bf16[256,576]{1,0:T(8,128)(2,1)S(1)} %bitcast_select_fusion.grad_ref.refs_9_, ...), custom_call_target="tpu_custom_call" | custom-call | tf_op jit(solution)/shard_map/layer_backward/pallas_call | solution.py:249
  208.0 10.1 %collective-permute-done.3 = bf16[256,576]{1,0:T(8,128)(2,1)S(1)} collective-permute-done((bf16[256,576]{1,0:T(8,128)(2,1)S(1)}, bf16[256,576]{1,0:T(8,128)(2,1)S(1)}, u32[]{:S(2)}, u32[]{:S(2)}) %collective-permute-start.3) | collective-permute-done | bytes 294944 | tf_op jit(solution)/shard_map/ppermute | solution.py:345
  218.2 14.2 %layer_backward.5 = (bf16[256,576]{1,0:T(8,128)(2,1)S(1)}, bf16[256,768]{1,0:T(8,128)(2,1)S(1)}, bf16[256,256]{1,0:T(8,128)(2,1)S(1)}, bf16[256,576]{1,0:T(8,128...) custom-call(bf16[256,576]{1,0:T(8,128)(2,1)S(1)} %broadcast_select_fusion.grad_ref.refs_19_, ...), custom_call_target="tpu_custom_call" | custom-call | tf_op jit(solution)/shard_map/layer_backward/pallas_call | solution.py:249
  233.1 9.9 %weight_grads.1 = (bf16[640,1536]{1,0:T(8,128)(2,1)}, bf16[640,1536]{1,0:T(8,128)(2,1)}, bf16[640,1536]{1,0:T(8,128)(2,1)}, bf16[1536,576]{1,0:T(8,128)(2,1)}) custom-call(bf16[256,640]{1,0:T(8,128)(2,1)S(1)} %get-tuple-element.67.refs_0_, bf16[256,640]{1,0:T(8,128)(2,1)S(1)} %get-tuple-element.68.refs_1_, bf16[256,640]{1,0:T(8,128)(2,1)S(1)} %get-tuple-element.69.refs_2_, ...), custom_call_target="tpu_custom_call" | custom-call | tf_op jit(solution)/shard_map/weight_grads/pallas_call | solution.py:373
  243.1 5.2 %reshape.106 = bf16[16,36,1536]{2,1,0:T(8,128)(2,1)} reshape(bf16[1536,576]{1,0:T(8,128)(2,1)} %get-tuple-element.88) | data formatting | bytes 3538944 | tf_op jit(solution)/shard_map/reshape | solution.py:306
  248.3 1.8 pad_bitcast_fusion
  251.0 5.4 %pad_maximum_fusion = bf16[16,4,40,1536]{3,2,0,1:T(8,128)(2,1)} fusion(bf16[16,1,40,1536]{3,2,0,1:T(8,128)(2,1)S(1)} %pad_bitcast_fusion, bf16[16,1,40,1536]{3,2,0,1:T(8,128)(2,1)} %bitcast.88, bf16[16,1,40,1536]{3,2,0,1:T(8,128)(2,1)S(1)} %bitcast.87, bf16[16,1,40,1536]{3,2,0,1:T(8,128)(2,1)S(1)} %bitcast.86), kind=kLoop, calls=%fused_computation | loop fusion | flops 11796480 | bytes 15728640 | tf_op jit(solution)/shard_map/stack | solution.py:307
  256.4 7.2 %copy.33 = bf16[16,4,40,1536]{3,2,1,0:T(8,128)(2,1)} copy(bf16[16,4,40,1536]{3,2,0,1:T(8,128)(2,1)} %pad_maximum_fusion) | data formatting | bytes 15728640 | tf_op jit(solution)/shard_map/stack | solution.py:307
  267.1 30.2 %psum.7 = f32[2,576]{1,0:T(2,128)S(1)} all-reduce(f32[2,576]{1,0:T(2,128)S(1)} %add.46), channel_id=1, replica_groups=mesh['section'=2,'dp'=16] {'dp'}, use_global_device_ids=true, to_apply=%region_2.3 | all-reduce | flops 1152 | bytes 9216 | tf_op jit(solution)/shard_map/psum | solution.py:379
  297.9 58.8 %reduce-scatter.2.cloned.1.call-done = bf16[160,1536]{1,0:T(8,128)(2,1)} async-done(((bf16[2560,1536]{1,0:T(8,128)(2,1)}), bf16[160,1536]{1,0:T(8,128)(2,1)}) %reduce-scatter.2.cloned.1.call-update) | async-done | bytes 491536 | tf_op jit(solution)/shard_map/reduce_scatter | solution.py:309
  (152 shorter events, 48.1 us)
Async XLA Ops:
  7.2 84.9 %all-gather.2.cloned.1.call-start = ((), (), s32[]{:S(2)}) async-start(), calls=%async_computation.1 | async-start | bytes 8355840 | tf_op jit(solution)/shard_map/all_gather | solution.py:284
  9.0 9.3 %copy-start.43 = (s32[2,1,256]{2,1,0:T(1,128)S(1)}, s32[2,1,256]{2,1,0:T(1,128)}, u32[]{:S(2)}) copy-start(s32[2,1,256]{2,1,0:T(1,128)} %param.13) | copy-start | bytes 6148
  9.0 9.3 %copy-start.41 = (bf16[2,256,576]{1,2,0:T(8,128)(2,1)S(1)}, bf16[2,256,576]{1,2,0:T(8,128)(2,1)}, u32[]{:S(2)}) copy-start(bf16[2,256,576]{1,2,0:T(8,128)(2,1)} %param.12) | copy-start | bytes 1769476
  17.7 339.0 %reduce-scatter.2.cloned.1.call-start = ((), (), s32[]{:S(2)}) async-start(), calls=%async_computation.2 | async-start | bytes 8355840 | tf_op jit(solution)/shard_map/reduce_scatter | solution.py:309
  23.1 82.8 %copy-start.1 = (bf16[576,640]{1,0:T(8,128)(2,1)}, bf16[576,640]{1,0:T(8,128)(2,1)S(1)}, u32[]{:S(2)}) copy-start(bf16[576,640]{1,0:T(8,128)(2,1)S(1)} %fusion.place_ref) | copy-start | bytes 2211844
  120.3 11.1 %collective-permute-start = (bf16[256,576]{1,0:T(8,128)(2,1)}, bf16[256,576]{1,0:T(8,128)(2,1)S(1)}, u32[]{:S(2)}, u32[]{:S(2)}) collective-permute-start(bf16[256,576]{1,0:T(8,128)(2,1)} %layer_forward.3), channel_id=1, source_target_pairs={{0,16},{1,17},{2,18},{3,19},{4,20},{5,21},{6,22},{7,23},{8,24},{9,... | collective-permute-start | bytes 884744 | tf_op jit(solution)/shard_map/ppermute | solution.py:342
  134.6 18.9 %copy-start.42 = (bf16[2,256,576]{1,2,0:T(8,128)(2,1)S(1)}, bf16[2,256,576]{1,2,0:T(8,128)(2,1)}, u32[]{:S(2)}) copy-start(bf16[2,256,576]{1,2,0:T(8,128)(2,1)} %param.23) | copy-start | bytes 1769476
  134.6 21.0 %copy-start.4 = (f32[256,128]{1,0:T(8,128)S(1)}, f32[256,128]{1,0:T(8,128)}, u32[]{:S(2)}) copy-start(f32[256,128]{1,0:T(8,128)} %get-tuple-element.135.cos_ref) | copy-start | bytes 393220
  134.6 21.0 %copy-start.7 = (f32[256,128]{1,0:T(8,128)S(1)}, f32[256,128]{1,0:T(8,128)}, u32[]{:S(2)}) copy-start(f32[256,128]{1,0:T(8,128)} %get-tuple-element.132.sin_ref) | copy-start | bytes 393220
  148.2 25.2 %copy-start.9 = (bf16[256,768]{1,0:T(8,128)(2,1)}, bf16[256,768]{1,0:T(8,128)(2,1)S(1)}, u32[]{:S(2)}) copy-start(bf16[256,768]{1,0:T(8,128)(2,1)S(1)} %get-tuple-element.53.qk_ref) | copy-start | bytes 1179652
  148.2 7.4 %copy-start.2 = (bf16[576,640]{1,0:T(8,128)(2,1)S(1)}, bf16[576,640]{1,0:T(8,128)(2,1)}, u32[]{:S(2)}) copy-start(bf16[576,640]{1,0:T(8,128)(2,1)} %copy-done.1) | copy-start | bytes 2211844
  148.2 28.0 %collective-permute-start.1 = (bf16[256,576]{1,0:T(8,128)(2,1)}, bf16[256,576]{1,0:T(8,128)(2,1)}, u32[]{:S(2)}, u32[]{:S(2)}) collective-permute-start(bf16[256,576]{1,0:T(8,128)(2,1)} %get-tuple-element.51), channel_id=1, source_target_pairs={{0,16},{1,17},{2,18},{3,19},{4,20},{5,21},{6,22},{7,23},{8,24},{9,... | collective-permute-start | bytes 884744 | tf_op jit(solution)/shard_map/ppermute | solution.py:342
  173.4 17.8 %collective-permute-start.2 = (bf16[256,576]{1,0:T(8,128)(2,1)}, bf16[256,576]{1,0:T(8,128)(2,1)}, u32[]{:S(2)}, u32[]{:S(2)}) collective-permute-start(bf16[256,576]{1,0:T(8,128)(2,1)} %layer_backward.3), channel_id=1, source_target_pairs={{16,0},{17,1},{18,2},{19,3},{20,4},{21,5},{22,6},{23,7},{24,8},{25... | collective-permute-start | bytes 884744 | tf_op jit(solution)/shard_map/ppermute | solution.py:345
  179.5 12.7 %copy-start.12 = (f32[256,128]{1,0:T(8,128)S(1)}, f32[256,128]{1,0:T(8,128)}, u32[]{:S(2)}) copy-start(f32[256,128]{1,0:T(8,128)} %get-tuple-element.134.cos_ref) | copy-start | bytes 393220
  179.5 12.7 %copy-start.14 = (f32[256,128]{1,0:T(8,128)S(1)}, f32[256,128]{1,0:T(8,128)}, u32[]{:S(2)}) copy-start(f32[256,128]{1,0:T(8,128)} %get-tuple-element.131.sin_ref) | copy-start | bytes 393220
  192.2 25.8 %copy-start.5 = (f32[256,128]{1,0:T(8,128)S(1)}, f32[256,128]{1,0:T(8,128)}, u32[]{:S(2)}) copy-start(f32[256,128]{1,0:T(8,128)} %get-tuple-element.135.cos_ref) | copy-start | bytes 393220
  192.3 25.8 %copy-start.8 = (f32[256,128]{1,0:T(8,128)S(1)}, f32[256,128]{1,0:T(8,128)}, u32[]{:S(2)}) copy-start(f32[256,128]{1,0:T(8,128)} %get-tuple-element.132.sin_ref) | copy-start | bytes 393220
  192.3 25.8 %copy-start.10 = (bf16[256,768]{1,0:T(8,128)(2,1)S(1)}, bf16[256,768]{1,0:T(8,128)(2,1)}, u32[]{:S(2)}) copy-start(bf16[256,768]{1,0:T(8,128)(2,1)} %copy-done.9) | copy-start | bytes 1179652
  192.3 25.8 %copy-start.18 = (bf16[256,192]{1,0:T(8,128)(2,1)S(1)}, bf16[256,192]{1,0:T(8,128)(2,1)}, u32[]{:S(2)}) copy-start(bf16[256,192]{1,0:T(8,128)(2,1)} %copy-done.16) | copy-start | bytes 294916
  192.3 25.8 %copy-start.21 = (f32[256,128]{1,0:T(8,128)S(1)}, f32[256,128]{1,0:T(8,128)}, u32[]{:S(2)}) copy-start(f32[256,128]{1,0:T(8,128)} %copy-done.19) | copy-start | bytes 393220
  206.7 11.4 %collective-permute-start.3 = (bf16[256,576]{1,0:T(8,128)(2,1)S(1)}, bf16[256,576]{1,0:T(8,128)(2,1)S(1)}, u32[]{:S(2)}, u32[]{:S(2)}) collective-permute-start(bf16[256,576]{1,0:T(8,128)(2,1)S(1)} %get-tuple-element.65), channel_id=1, source_target_pairs={{16,0},{17,1},{18,2},{19,3},{20,4},{21,5},{22,6},{23,7},{24,8},{25... | collective-permute-start | bytes 884744 | tf_op jit(solution)/shard_map/ppermute | solution.py:345
  218.1 15.0 %copy-start.26 = (bf16[256,640]{1,0:T(8,128)(2,1)S(1)}, bf16[256,640]{1,0:T(8,128)(2,1)}, u32[]{:S(2)}) copy-start(bf16[256,640]{1,0:T(8,128)(2,1)} %copy-done.25) | copy-start | bytes 983044
  218.1 15.0 %copy-start.28 = (bf16[256,640]{1,0:T(8,128)(2,1)S(1)}, bf16[256,640]{1,0:T(8,128)(2,1)}, u32[]{:S(2)}) copy-start(bf16[256,640]{1,0:T(8,128)(2,1)} %copy-done.27) | copy-start | bytes 983044
  218.2 15.0 %copy-start.30 = (bf16[256,640]{1,0:T(8,128)(2,1)S(1)}, bf16[256,640]{1,0:T(8,128)(2,1)}, u32[]{:S(2)}) copy-start(bf16[256,640]{1,0:T(8,128)(2,1)} %copy-done.29) | copy-start | bytes 983044
  (26 other events, 45.1 us)
Sparse Core Ops, SparseCore 0:
  17.8 74.2 all-gather.1
  263.8 92.8 reduce-scatter.1

commit v2 on v1

v2 whole, which is shorter than its diff:
```python
import functools
import math

import jax
import jax.numpy as jnp
from jax import lax
from jax.experimental import pallas as pl
from jax.experimental.pallas import tpu as pltpu
from jax.sharding import PartitionSpec as P

D = 576
HEADS = 9
KV_HEADS = 3
HEAD = 64
FF = 1536
TOK_MB = 256
QW = HEADS * HEAD
KVW = KV_HEADS * HEAD
REP = HEADS // KV_HEADS

EPS = 1e-05
THETA = 100000.0
NEG = -1000000000.0

PAD = 640
COL_K = QW
COL_O = QW + KVW
COL_V = COL_O + D
COL_VX = 1280
SKIP_V = COL_V - COL_VX

BF = jnp.bfloat16
F32 = jnp.float32

PARAMS = pltpu.CompilerParams(vmem_limit_bytes=60 * 1024 * 1024)


def dot(left, right):
    return lax.dot_general(left, right, (((1,), (0,)), ((), ())), preferred_element_type=F32)


def dot_nt(left, right):
    return lax.dot_general(left, right, (((1,), (1,)), ((), ())), preferred_element_type=F32)


def dot_tn(left, right):
    return lax.dot_general(left, right, (((0,), (0,)), ((), ())), preferred_element_type=F32)


def spread(rows, place):
    return dot(rows, place).astype(BF)


def collect(rows, place):
    high = rows.astype(BF)
    low = (rows - high.astype(F32)).astype(BF)
    return dot_nt(high, place) + dot_nt(low, place)


def turned(tile):
    lane = lax.broadcasted_iota(jnp.int32, tile.shape, 1)
    return jnp.where(lane % HEAD < HEAD // 2, pltpu.roll(tile, 128 - HEAD // 2, 1), pltpu.roll(tile, HEAD // 2, 1))


def inv_rms(stream):
    return lax.rsqrt(jnp.mean(stream * stream, -1, keepdims=True) + EPS)


def norm_back(stream, gain_row, grad_normed):
    scale_r = inv_rms(stream)
    weighted = grad_normed * gain_row
    grad_stream = scale_r * weighted - stream * scale_r**3 * jnp.mean(
        stream * weighted, -1, keepdims=True
    )
    grad_gain = jnp.sum(grad_normed * stream * scale_r, 0, keepdims=True)
    return (grad_stream, grad_gain)


CHUNK = 512
CHUNKS = FF // CHUNK
HALF = TOK_MB // 2
GROUPS = 16
EACH = PAD // GROUPS
EACH_FF = FF // GROUPS
DV = QW + D + 2 * KVW - COL_VX

ANY = pl.BlockSpec(memory_space=pl.ANY)
SMEM = pl.BlockSpec(memory_space=pltpu.SMEM)
VMEM = pl.BlockSpec(memory_space=pltpu.VMEM)


def shape(*dims, dtype=BF):
    return jax.ShapeDtypeStruct(dims, dtype)


class Names:
    def __getattr__(self, name):
        return name


N = Names()


STORED = dict(
    na=shape(TOK_MB, PAD),
    qk=shape(TOK_MB, COL_O),
    v=shape(TOK_MB, KVW),
    lse=shape(TOK_MB, 128, dtype=F32),
    mx=shape(TOK_MB, PAD),
    mid=shape(TOK_MB, D, dtype=F32),
    nb=shape(TOK_MB, PAD),
    gate=shape(TOK_MB, FF, dtype=F32),
    up=shape(TOK_MB, FF, dtype=F32),
    act=shape(TOK_MB, FF),
)
FOR_BACK = (N.gate, N.up, N.mid, N.qk, N.v, N.lse)
KEPT = dict(
    dqk=shape(TOK_MB, COL_O),
    dv=shape(TOK_MB, DV),
    gattn=shape(TOK_MB, D),
    dg=shape(TOK_MB, FF),
    du=shape(TOK_MB, FF),
)
INPUTS = dict(
    agu=shape(3, PAD, FF),
    c_lo=shape(GROUPS, EACH_FF // 2, D),
    c_hi=shape(GROUPS, EACH_FF // 2, D),
    place=shape(D, PAD),
    cos=shape(2, TOK_MB, 128, dtype=F32),
    sin=shape(2, TOK_MB, 128, dtype=F32),
    mask=shape(2, TOK_MB, TOK_MB, dtype=F32),
)
HELD = dict(
    att=shape(PAD, FF),
    gw=shape(PAD, FF),
    uw=shape(PAD, FF),
    down=shape(GROUPS, EACH_FF, D),
    place=shape(D, PAD),
    cos=shape(TOK_MB, 128, dtype=F32),
    sin=shape(TOK_MB, 128, dtype=F32),
    mask=shape(TOK_MB, TOK_MB, dtype=F32),
    x=shape(TOK_MB, D),
    g=shape(TOK_MB, D),
)


class Copies:
    def __init__(self, sems):
        self.sems, self.count, self.open = sems, 0, {}

    def start(self, name, source, target):
        copy = pltpu.make_async_copy(source, target, self.sems.at[self.count])
        self.count += 1
        self.open.setdefault(name, []).append(copy)
        copy.start()

    def start_either(self, name, take_one, one, two, target):
        first = pltpu.make_async_copy(one, target, self.sems.at[self.count])
        second = pltpu.make_async_copy(two, target, self.sems.at[self.count])
        self.count += 1
        self.open.setdefault(name, []).append(first)

        @pl.when(take_one)
        def _():
            first.start()

        @pl.when(jnp.logical_not(take_one))
        def _():
            second.start()

    def wait(self, *names):
        for name in names:
            for copy in self.open.pop(name, ()):
                copy.wait()

    def wait_all(self):
        self.wait(*list(self.open))


def blocks_of_rows():
    return ((0, HALF, HALF), (HALF, TOK_MB, TOK_MB))


def forward(held, kept, copies, ga_ref, gb_ref, note):
    copies.wait(N.x, N.place)
    place = held[N.place][...]
    stream = held[N.x][...].astype(F32)
    normed_a = spread((stream * inv_rms(stream) * ga_ref[...]).astype(BF), place)
    note(N.na, normed_a)
    copies.wait(N.att, N.cos, N.sin)
    raw = dot(normed_a, held[N.att][:, :COL_O])
    cosine, sine = held[N.cos][...], held[N.sin][...]
    tiles = []
    lane = lax.broadcasted_iota(jnp.int32, (TOK_MB, 128), 1)
    for j in range(COL_O // 128):
        tile = raw[:, 128 * j : 128 * (j + 1)]
        tile = (tile * cosine + turned(tile) * sine).astype(BF)
        if 128 * (j + 1) <= QW:
            tile = tile * jnp.asarray(HEAD ** (-0.5), BF)
        elif 128 * j < QW:
            tile = jnp.where(lane < QW - 128 * j, tile.astype(F32) * HEAD ** (-0.5), tile.astype(F32)).astype(BF)
        tiles.append(tile)
    qk = jnp.concatenate(tiles, 1)
    note(N.qk, qk)
    value = dot(normed_a, held[N.att][:, COL_VX:])[:, SKIP_V:].astype(BF)
    note(N.v, value)
    copies.wait(N.mask)
    mixed = []
    for h in range(HEADS):
        kv = h // REP
        key = qk[:, COL_K + HEAD * kv : COL_K + HEAD * (kv + 1)]
        val = value[:, HEAD * kv : HEAD * (kv + 1)]
        parts = []
        for low, high, keys in blocks_of_rows():
            query = qk[low:high, HEAD * h : HEAD * (h + 1)]
            scores = jnp.where(held[N.mask][low:high, :keys] > 0.5, dot_nt(query, key[:keys]), NEG)
            row_max = jnp.max(scores, -1, keepdims=True)
            terms = jnp.exp(scores - row_max)
            total = jnp.sum(terms, -1, keepdims=True)
            attend = (terms * (1.0 / total)).astype(BF)
            parts.append(dot(attend, val[:keys]).astype(BF))
            if kept is not None:
                kept[N.lse][low:high, h : h + 1] = row_max + jnp.log(total)
        mixed.append(jnp.concatenate(parts, 0))
    note(N.lse, None)
    mixed_p = spread(jnp.concatenate(mixed, 1), place)
    note(N.mx, mixed_p)
    middle = stream + dot(mixed_p, held[N.att][:, COL_O : COL_O + D])
    note(N.mid, middle)
    normed_b = spread((middle * inv_rms(middle) * gb_ref[...]).astype(BF), place)
    note(N.nb, normed_b)
    copies.wait(N.gw, N.uw, N.down)
    result = middle
    for c in range(0, FF, CHUNK):
        gate = dot(normed_b, held[N.gw][:, c : c + CHUNK])
        up = dot(normed_b, held[N.uw][:, c : c + CHUNK])
        act = (gate * jax.nn.sigmoid(gate) * up).astype(BF)
        result = result + dot(act, down_of(held)[c : c + CHUNK])
        if kept is not None:
            kept[N.gate][:, c : c + CHUNK] = gate
            kept[N.up][:, c : c + CHUNK] = up
            kept[N.act][:, c : c + CHUNK] = act
    note(N.gate, None)
    note(N.up, None)
    note(N.act, None)
    return result.astype(BF)


def down_of(held):
    return held[N.down][...].reshape(FF, D)


def backward(held, kept, copies, ga_ref, gb_ref, note):
    copies.wait(N.g, N.down)
    grad_low = held[N.g][...]
    grad_out = grad_low.astype(F32)
    back_p = jnp.zeros((TOK_MB, PAD), F32)
    down = down_of(held)
    for c in range(0, FF, CHUNK):
        grad_act = dot_nt(grad_low, down[c : c + CHUNK])
        copies.wait(N.gate + str(c), N.up + str(c))
        gate = kept[N.gate][:, c : c + CHUNK]
        up = kept[N.up][:, c : c + CHUNK]
        sig = jax.nn.sigmoid(gate)
        acts = grad_act * sig
        d_gate = (acts * up * (1.0 + gate * (1.0 - sig))).astype(BF)
        d_up = (acts * gate).astype(BF)
        note(N.dg, d_gate, c)
        note(N.du, d_up, c)
        copies.wait(N.gw, N.uw)
        back_p = back_p + dot_nt(d_gate, held[N.gw][:, c : c + CHUNK]) + dot_nt(d_up, held[N.uw][:, c : c + CHUNK])
    copies.wait(N.place, N.mid, N.att)
    place = held[N.place][...]
    back_b, gain_b = norm_back(kept[N.mid][...], gb_ref[...], collect(back_p, place))
    grad_middle = grad_out + back_b
    grad_attn = grad_middle.astype(BF)
    note(N.gattn, grad_attn)
    grad_mixed = dot_nt(dot_nt(grad_attn, held[N.att][:, COL_O : COL_O + D]).astype(BF), place).astype(BF)
    copies.wait(N.qk, N.v, N.lse, N.mask, N.cos, N.sin, N.x)
    d_query, d_key, d_value = [], [], []
    for kv in range(KV_HEADS):
        key = kept[N.qk][:, COL_K + HEAD * kv : COL_K + HEAD * (kv + 1)]
        value = kept[N.v][:, HEAD * kv : HEAD * (kv + 1)]
        sums_k, sums_v = [None, None], [None, None]
        for h in range(kv * REP, (kv + 1) * REP):
            parts = []
            for at, (low, high, keys) in enumerate(blocks_of_rows()):
                query = kept[N.qk][low:high, HEAD * h : HEAD * (h + 1)]
                grad_h = grad_mixed[low:high, HEAD * h : HEAD * (h + 1)]
                scores = jnp.where(held[N.mask][low:high, :keys] > 0.5, dot_nt(query, key[:keys]), NEG)
                attend = jnp.exp(scores - kept[N.lse][low:high, h : h + 1])
                grad_attend = dot_nt(grad_h, value[:keys])
                inner = jnp.sum(attend * grad_attend, -1, keepdims=True)
                grad_scores = (attend * (grad_attend - inner)).astype(BF)
                part_v = dot_tn(attend.astype(BF), grad_h)
                part_k = dot_tn(grad_scores, query)
                sums_v[at] = part_v if sums_v[at] is None else sums_v[at] + part_v
                sums_k[at] = part_k if sums_k[at] is None else sums_k[at] + part_k
                parts.append(dot(grad_scores, key[:keys]) * HEAD ** (-0.5))
            d_query.append(jnp.concatenate(parts, 0))
        d_key.append(jnp.concatenate([sums_k[0] + sums_k[1][:HALF], sums_k[1][HALF:]], 0))
        d_value.append(jnp.concatenate([sums_v[0] + sums_v[1][:HALF], sums_v[1][HALF:]], 0).astype(BF))
    raw = jnp.concatenate(d_query + d_key, 1)
    cosine, sine = held[N.cos][...], held[N.sin][...]
    tiles = []
    for j in range(COL_O // 128):
        tile = raw[:, 128 * j : 128 * (j + 1)]
        tiles.append((tile * cosine - turned(tile) * sine).astype(BF))
    d_qk = jnp.concatenate(tiles, 1)
    d_v = jnp.concatenate([jnp.zeros((TOK_MB, SKIP_V), BF)] + d_value, 1)
    note(N.dqk, d_qk)
    note(N.dv, d_v)
    back_p = dot_nt(d_qk, held[N.att][:, :COL_O]) + dot_nt(d_v, held[N.att][:, COL_VX:])
    back_a, gain_a = norm_back(held[N.x][...].astype(F32), ga_ref[...], collect(back_p, place))
    return (grad_middle + back_a).astype(BF), gain_a, gain_b


SLOTS = dict(
    lead=(N.forward,),
    both=(N.forward, N.backward, N.store),
    ahead=(N.forward, N.store),
    behind=(N.backward, N.keep),
)


def layer_kernel(name, micro, names, refs):
    does = SLOTS[name]
    ref = dict(zip(names, refs))
    held = {key: ref["held_" + key] for key in HELD if "held_" + key in ref}
    kept = {key: ref["kept_" + key] for key in STORED if "kept_" + key in ref} or None
    section = ref[N.coords][3]
    index = {N.zero: 0, N.one: 1, N.same: section, N.other: 1 - section}[micro]
    copies = Copies(ref[N.sems])

    def bring(key):
        copies.start(key, ref[key].at[index], held[key])

    def bring_x():
        if N.arrived in ref:
            copies.start_either(N.x, section == 0, ref[N.tokens].at[index], ref[N.arrived], held[N.x])
        else:
            copies.start(N.x, ref[N.tokens].at[index], held[N.x])

    def bring_weights(order):
        for key in order:
            if key == N.down:
                copies.start(key, ref[N.c_lo], held[N.down].at[:, : EACH_FF // 2])
                copies.start(key, ref[N.c_hi], held[N.down].at[:, EACH_FF // 2 :])
            elif key == N.place:
                copies.start(key, ref[N.place], held[N.place])
            else:
                copies.start(key, ref[N.agu].at[(N.att, N.gw, N.uw).index(key)], held[key])

    def bring_g():
        if N.arrived_grad in ref:
            copies.start_either(N.g, section == 0, ref[N.arrived_grad], ref[N.out_grad].at[index], held[N.g])
        else:
            copies.start(N.g, ref[N.out_grad].at[index], held[N.g])

    if N.forward in does:
        bring_x()
        bring_weights([N.place, N.att])
        bring(N.cos)
        bring(N.sin)
        bring(N.mask)
        bring_weights([N.gw, N.uw, N.down])
        if N.backward in does:
            bring_g()
    else:
        bring_g()
        bring_weights([N.down])
        for c in range(0, FF, CHUNK):
            for key in (N.gate, N.up):
                copies.start(key + str(c), ref["stored_" + key].at[:, c : c + CHUNK], kept[key].at[:, c : c + CHUNK])
        bring_weights([N.gw, N.uw, N.place])
        copies.start(N.mid, ref[N.stored_mid], kept[N.mid])
        bring_weights([N.att])
        for key in (N.qk, N.v, N.lse):
            copies.start(key, ref["stored_" + key], kept[key])
        bring(N.mask)
        bring(N.cos)
        bring(N.sin)
        bring_x()

    def note_stored(key, value, column=None):
        if N.store in does:
            if value is not None:
                kept[key][...] = value
            copies.start("out_" + key, kept[key], ref["store_" + key])

    def note_kept(key, value, column=None):
        if N.keep in does:
            if column is None:
                ref["made_" + key][...] = value
            else:
                ref["made_" + key][:, column : column + CHUNK] = value
            if column in (None, FF - CHUNK):
                copies.start("out_" + key, ref["made_" + key], ref["keep_" + key])

    if N.forward in does:
        ref[N.out][...] = forward(held, kept, copies, ref[N.ga], ref[N.gb], note_stored)
    if N.backward in does:
        grad, gain_a, gain_b = backward(held, kept, copies, ref[N.ga], ref[N.gb], note_kept)
        ref[N.in_grad][...] = grad
        if N.keep in does:
            ref[N.gains][0:1, :] = gain_a
            ref[N.gains][1:2, :] = gain_b
    copies.wait_all()


def run_layer(name, micro, common, tokens, arrived=None, out_grad=None, arrived_grad=None, stored=None):
    does = SLOTS[name]
    operands = dict(coords=common[N.coords], tokens=tokens, ga=common[N.ga], gb=common[N.gb])
    operands.update({key: common[key] for key in INPUTS})
    specs = dict(coords=SMEM, ga=VMEM, gb=VMEM)
    if arrived is not None:
        operands[N.arrived] = arrived
    if N.backward in does:
        operands[N.out_grad] = out_grad
        if arrived_grad is not None:
            operands[N.arrived_grad] = arrived_grad
    if stored is not None:
        operands.update({"stored_" + key: stored[key] for key in FOR_BACK})
    outs, out_specs = {}, []
    if N.forward in does:
        outs[N.out] = shape(TOK_MB, D)
    if N.backward in does:
        outs[N.in_grad] = shape(TOK_MB, D)
    if N.keep in does:
        outs[N.gains] = shape(2, D, dtype=F32)
        outs.update({"keep_" + key: KEPT[key] for key in KEPT})
    if N.store in does:
        outs.update({"store_" + key: STORED[key] for key in STORED})
    out_specs = [ANY if key.startswith(("store_", "keep_")) else VMEM for key in outs]
    scratch = {"held_" + key: pltpu.VMEM(h.shape, h.dtype) for key, h in HELD.items() if key != N.g or N.backward in does}
    if name != N.lead:
        hold = STORED if N.forward in does else FOR_BACK
        scratch.update({"kept_" + key: pltpu.VMEM(STORED[key].shape, STORED[key].dtype) for key in hold})
    if N.keep in does:
        scratch.update({"made_" + key: pltpu.VMEM(KEPT[key].shape, BF) for key in KEPT})
    scratch[N.sems] = pltpu.SemaphoreType.DMA((40,))
    names = list(operands) + list(outs) + list(scratch)

    def kernel(*refs):
        layer_kernel(name, micro, names, refs)

    results = pl.pallas_call(
        kernel,
        out_shape=list(outs.values()),
        in_specs=[specs.get(key, ANY) for key in operands],
        out_specs=out_specs,
        scratch_shapes=list(scratch.values()),
        compiler_params=PARAMS,
        name="layer_" + name,
    )(*operands.values())
    return dict(zip(outs, results))


PAIRS = (N.act, N.g, N.nb, N.dg, N.du, N.mx, N.gattn, N.na, N.dqk, N.dv)


def slab_of(block):
    return jnp.concatenate(
        [
            jnp.concatenate([block[8 * i : 8 * i + 8, 128 * j : 128 * j + 128] for i in range(EACH_FF // 8)], 1)
            for j in range(PAD // 128)
        ],
        0,
    )


def block_of(slab):
    tiles = slab.reshape(slab.shape[:-2] + (PAD // 128, 8, EACH_FF // 8, 128))
    return jnp.moveaxis(tiles, -2, -4).swapaxes(-3, -2).reshape(slab.shape[:-2] + (EACH_FF, PAD))


def weights_kernel(names, refs):
    ref = dict(zip(names, refs))
    copies = Copies(ref[N.sems])
    own_z, own_x, own_c, section = (ref[N.coords][i] for i in range(4))
    for key in PAIRS:
        for at in range(2):
            target = ref["in_" + key].at[pl.ds(TOK_MB * at, TOK_MB)]
            if key == N.g:
                copies.start_either(
                    key, section == 0, ref["grad_%d" % at], ref[N.out_grad].at[section if at == 0 else 1 - section], target
                )
            else:
                copies.start(key, ref["%s_%d" % (key, at)], target)

    def put_pairs(keep_ref, send_ref, at, columns, blocks, pair):
        for one, two in zip(blocks[::2], blocks[1::2]):
            far, across = lax.rem(pair // 2 - own_z + 4, 4), lax.rem(pair % 2 + own_x, 2)
            index = (across, far) + at + (slice(None), columns)
            keep_ref[index] = jnp.where(own_c == 0, one, two).astype(BF)
            send_ref[index] = jnp.where(own_c == 0, two, one).astype(BF)
            pair += 1

    def put(keep_ref, send_ref, at, columns, rows):
        put_pairs(keep_ref, send_ref, at, columns, jnp.split(rows, GROUPS), 0)

    copies.wait(N.act, N.g)
    grad_down = jnp.concatenate([ref[N.in_g][...], jnp.zeros((2 * TOK_MB, PAD - D), BF)], 1)
    step = 4 * EACH_FF
    for c in range(0, FF, step):
        slabs = [slab_of(piece) for piece in jnp.split(dot_tn(ref[N.in_act][:, c : c + step], grad_down), 4)]
        put_pairs(ref[N.keep_m], ref[N.send_m], (3,), slice(0, FF), slabs, c // step * 2)
    copies.wait(N.nb, N.dg, N.du)
    normed_b = ref[N.in_nb][...]
    for at, key in ((1, N.dg), (2, N.du)):
        for c in range(0, FF, CHUNK):
            put(ref[N.keep_m], ref[N.send_m], (at,), slice(c, c + CHUNK), dot_tn(normed_b, ref["in_" + key][:, c : c + CHUNK]))
    copies.wait(N.mx, N.gattn, N.na, N.dqk, N.dv)
    normed_a, mixed = ref[N.in_na][...], ref[N.in_mx][...]
    put(ref[N.keep_m], ref[N.send_m], (0,), slice(0, COL_O), dot_tn(normed_a, ref[N.in_dqk][...]))
    put(ref[N.keep_m], ref[N.send_m], (0,), slice(COL_O, COL_VX), dot_tn(mixed, ref[N.in_gattn][:, : COL_VX - COL_O]))
    grad_o = dot_tn(mixed, ref[N.in_gattn][:, COL_VX - COL_O :])
    grad_o = jnp.concatenate([grad_o, jnp.zeros((PAD, KVW), F32)], 1)
    put(ref[N.keep_m], ref[N.send_m], (0,), slice(COL_VX, FF), dot_tn(normed_a, ref[N.in_dv][...]) + grad_o)
    copies.start(N.out, ref[N.send_m], ref[N.out_send_m])
    copies.start(N.out, ref[N.keep_m], ref[N.out_keep_m])
    copies.wait_all()


def run_weights(coords, rows, grads, out_grad):
    operands = dict(coords=coords, out_grad=out_grad)
    for at in range(2):
        operands["grad_%d" % at] = grads[at]
        operands.update({"%s_%d" % (key, at): rows[at][key] for key in PAIRS if key != N.g})
    main = shape(2, 4, 4, EACH, FF)
    outs = dict(out_keep_m=main, out_send_m=main)
    columns = {key: (STORED | KEPT | {N.g: HELD[N.g]})[key].shape[1] for key in PAIRS}
    scratch = {"in_" + key: pltpu.VMEM((2 * TOK_MB, columns[key]), BF) for key in PAIRS}
    scratch.update({key[4:]: pltpu.VMEM(out.shape, BF) for key, out in outs.items()})
    scratch[N.sems] = pltpu.SemaphoreType.DMA((32,))
    names = list(operands) + list(outs) + list(scratch)

    def kernel(*refs):
        weights_kernel(names, refs)

    results = pl.pallas_call(
        kernel,
        out_shape=list(outs.values()),
        in_specs=[SMEM] + [ANY] * (len(operands) - 1),
        out_specs=[ANY] * len(outs),
        scratch_shapes=list(scratch.values()),
        compiler_params=PARAMS,
        name=N.weight_grads,
    )(*operands.values())
    return dict(zip(outs, results))


def make_tables(seg_row):
    count_t = seg_row.shape[0]
    order_idx = jnp.arange(count_t, dtype=jnp.int32)
    same_doc = seg_row[:, None] == seg_row[None, :]
    before = order_idx[None, :] < order_idx[:, None]
    positions = jnp.sum(jnp.where(same_doc & before, jnp.float32(1.0), jnp.float32(0.0)), axis=1)
    allowed = same_doc & (order_idx[None, :] <= order_idx[:, None])
    inv_freq = jnp.exp(jnp.arange(HEAD // 2, dtype=jnp.float32) * (-2.0 * math.log(THETA) / HEAD))
    angles = positions[:, None] * inv_freq[None, :]
    cosine, sine = jnp.cos(angles), jnp.sin(angles)
    cosine = jnp.concatenate([cosine] * 4, -1)
    sine = jnp.concatenate([-sine, sine] * 2, -1)
    return (cosine, sine, allowed.astype(F32))


def placement(rows_each, rows_padded):
    row = lax.broadcasted_iota(jnp.int32, (D, PAD), 0)
    col = lax.broadcasted_iota(jnp.int32, (D, PAD), 1)
    return (col == row + (row // rows_each) * (rows_padded - rows_each)).astype(BF)


def gather_weights(shard, owners):
    w_query, w_key, w_value, w_out, w_gate, w_up, w_down = shard
    if owners == GROUPS:
        rows = D // owners
        att = jnp.concatenate(
            [w_query.reshape(rows, QW), w_key.reshape(rows, KVW), w_out.reshape(rows, D), w_value.reshape(rows, KVW)], 1
        )
        packed = jnp.stack([att, w_gate.reshape(rows, FF), w_up.reshape(rows, FF)])
        packed = jnp.pad(packed, ((0, 0), (0, EACH - rows), (0, 0)))
        agu = lax.all_gather(packed, "dp", axis=1, tiled=True)
        w_down = w_down.reshape(EACH_FF, D)
        c_lo = lax.all_gather(w_down[: EACH_FF // 2], "dp", axis=0, tiled=False)
        c_hi = lax.all_gather(w_down[EACH_FF // 2 :], "dp", axis=0, tiled=False)
        return agu, c_lo, c_hi, placement(rows, EACH)
    w_query, w_key, w_value, w_out, w_gate, w_up, w_down = (
        lax.all_gather(member[0], "dp", axis=0, tiled=True) for member in shard
    )
    att = jnp.concatenate(
        [w_query.reshape(D, QW), w_key.reshape(D, KVW), w_out.reshape(QW, D), w_value.reshape(D, KVW)], 1
    )
    agu = jnp.pad(jnp.stack([att, w_gate.reshape(D, FF), w_up.reshape(D, FF)]), ((0, 0), (0, PAD - D), (0, 0)))
    down = w_down.reshape(GROUPS, EACH_FF, D)
    return agu, down[:, : EACH_FF // 2], down[:, EACH_FF // 2 :], placement(D, D)


def cut(att):
    return att[:, :QW], att[:, COL_K:COL_O], att[:, COL_V:], att[:, COL_O:COL_V]


def place_of(z, x, c):
    return (z * 2 + x) * 2 + c


PLACES = [(z, x, c) for z in range(4) for x in range(2) for c in range(2)]


def to_core(block):
    return lax.ppermute(block, "dp", [(place_of(z, x, c), place_of(z, x, 1 - c)) for z, x, c in PLACES])


def to_across(block):
    return lax.ppermute(block, "dp", [(place_of(z, x, c), place_of(z, 1 - x, c)) for z, x, c in PLACES])


def to_far(block, far):
    return lax.ppermute(block, "dp", [(place_of(z, x, c), place_of((z + far) % 4, x, c)) for z, x, c in PLACES])


def add(*terms):
    return sum(term.astype(F32) for term in terms)


def moved(value, dz, dx, dc):
    return lax.ppermute(value, "dp", [(place_of(z, x, c), place_of(z ^ dz, x ^ dx, c ^ dc)) for z, x, c in PLACES])


def sum_of_four(value, others):
    return (value + others[0]) + (others[1] + others[2])


def reduce_blocks(keep, send, gains):
    near = [moved(gains, 0, 0, 1), moved(gains, 0, 1, 0), moved(gains, 0, 1, 1)]
    got = to_core(send)
    got, near = lax.optimization_barrier((got, near))
    gains = sum_of_four(gains, near)
    wide = [moved(gains, 1, 0, 0), moved(gains, 2, 0, 0), moved(gains, 3, 0, 0)]
    blocks = {far: add(keep[1, far], got[1, far]).astype(BF) for far in range(4)}
    one, two = to_across(blocks[2]), to_across(blocks[1])
    one, wide = lax.optimization_barrier((one, wide))
    gains = sum_of_four(gains, wide)
    term_two = add(keep[0, 2], got[0, 2], one).astype(BF)
    term_two, last = lax.optimization_barrier((term_two, blocks[3]))
    far_two, three = to_far(term_two, 2), to_across(last)
    term_one = add(keep[0, 1], got[0, 1], two).astype(BF)
    term_one, last = lax.optimization_barrier((term_one, blocks[0]))
    far_one, four = to_far(term_one, 1), to_across(last)
    three, term_one = lax.optimization_barrier((three, term_one))
    far_three = to_far(add(keep[0, 3], got[0, 3], three).astype(BF), 3)
    return add(keep[0, 0], got[0, 0], four, far_two, far_one, far_three), gains


def scatter_grads(out, gains, owners):
    if owners == GROUPS:
        main, gains = reduce_blocks(out[N.out_keep_m], out[N.out_send_m], gains)
        rows = D // owners
        att, gate, up = main[0, :rows], main[1, :rows], main[2, :rows]
        down = block_of(main[3])[:, :D]
        return tuple(piece.reshape(1, -1) for piece in cut(att) + (gate, up, down)) + (gains[0:1], gains[1:2])
    main = jnp.stack([out[N.out_keep_m], out[N.out_send_m]]).transpose(3, 2, 1, 0, 4, 5).reshape(4, GROUPS, EACH, FF)
    down = block_of(main[3])[:, :, :D].reshape(FF, D)
    main = main[:3].reshape(3, PAD, FF)[:, :D]
    pieces = cut(main[0]) + (main[1], main[2], down)
    gains = lax.psum(gains, "dp")
    return tuple(
        lax.psum_scatter(piece.reshape(owners, -1), "dp", scatter_dimension=0, tiled=True).astype(F32) for piece in pieces
    ) + (gains[0:1], gains[1:2])


def shards(
    tokens,
    segments,
    w_query,
    w_key,
    w_value,
    w_out,
    w_gate,
    w_up,
    w_down,
    attn_gain,
    mlp_gain,
    out_grad,
):
    section = lax.axis_index("section")
    first = section == 0
    owners = lax.axis_size("dp")
    me = lax.axis_index("dp") if owners == GROUPS else 0
    coords = jnp.stack([me // 4, me // 2 % 2, me % 2, section, 0, 0, 0, 0]).astype(jnp.int32)
    agu, c_lo, c_hi, place = gather_weights((w_query, w_key, w_value, w_out, w_gate, w_up, w_down), owners)
    cosine, sine, mask = jax.vmap(make_tables)(segments[:, 0])
    agu, c_lo, c_hi, place, cosine, sine, mask, tokens, out_grad, coords = lax.optimization_barrier(
        (agu, c_lo, c_hi, place, cosine, sine, mask, tokens, out_grad, coords)
    )
    common = dict(
        agu=agu, c_lo=c_lo, c_hi=c_hi, place=place, cos=cosine, sin=sine, mask=mask, coords=coords, ga=attn_gain, gb=mlp_gain
    )

    def send_on(block):
        return lax.ppermute(block, "section", [(0, 1)])

    def send_back(block):
        return lax.ppermute(block, "section", [(1, 0)])

    def stored_of(outs):
        return {key: outs["store_" + key] for key in STORED}

    def rows_of(stored, outs):
        return stored | {key: outs["keep_" + key] for key in KEPT}

    lead_zero = run_layer(N.lead, N.zero, common, tokens)[N.out]
    arrived_zero = send_on(lead_zero)
    lead_one = run_layer(N.lead, N.one, common, tokens)[N.out]
    arrived_one = send_on(lead_one)
    two = run_layer(N.both, N.other, common, tokens, arrived_zero, out_grad)
    arrived_grad = send_back(two[N.in_grad])
    four = run_layer(N.ahead, N.same, common, tokens, arrived_one)
    stored_two, stored_four = stored_of(two), stored_of(four)
    five = run_layer(N.behind, N.same, common, tokens, arrived_one, out_grad, arrived_grad, stored_four)
    last_grad = send_back(five[N.in_grad])
    six = run_layer(N.behind, N.other, common, tokens, arrived_zero, out_grad, last_grad, stored_two)
    grads = run_weights(
        coords, (rows_of(stored_four, five), rows_of(stored_two, six)), (arrived_grad, last_grad), out_grad
    )
    shares = scatter_grads(grads, five[N.gains] + six[N.gains], owners)
    layer_out = jnp.stack([jnp.where(first, four[N.out], two[N.out]), jnp.where(first, two[N.out], four[N.out])])
    input_grad = jnp.stack([jnp.where(first, five[N.in_grad], six[N.in_grad]), jnp.where(first, six[N.in_grad], five[N.in_grad])])
    return (layer_out[None], input_grad[None], *shares)


def solution(mesh):
    weights = (P("section", "dp"),) * 7
    gains = (P("section", None),) * 2
    rows = P("section", None, "dp", None)
    return jax.shard_map(
        shards,
        mesh=mesh,
        in_specs=(P(None, "dp", None), P(None, "dp", None), *weights, *gains, P(None, "dp", None)),
        out_specs=(rows, rows, *weights, *gains),
        check_vma=False,
    )
```

time: 375 us -> 321 us (0.86)
  waiting for transfers between devices: 143 us -> 76.9 us
  local copies, waits for them, and re-layouts: 62.1 us -> 19.5 us
  blocking collectives: 30.2 us -> 56.7 us
  Pallas kernels: 87.2 us -> 103 us
  starting transfers between devices: 12.5 us -> 23.3 us
    reduce_scatter x1 -> x0, waiting for transfers between devices: 58.8 us -> none  [scatter_grads(): share = lax.psum_scatter(packed, 'dp', scatter_dimension=0, tiled=True)]
    all_gather x1, waiting for transfers between devices: 68.1 us -> 10.7 us  [gather_weights(): agu = lax.all_gather(packed, 'dp', axis=1, tiled=True)]
    all_gather x0 -> x2, blocking collectives: none -> 56.7 us  [the longest x1 29.4 us: gather_weights(): c_lo = lax.all_gather(w_down[:EACH_FF // 2], 'dp', axis=0, tiled=False)]
    ppermute x0 -> x14, waiting for transfers between devices: none -> 55.7 us  [the longest x3 25.1 us: to_far(): lax.ppermute(block, 'dp', [(place_of(z, x, c), place_of((z + far) % 4, x,...]
    psum x1 -> x0, blocking collectives: 30.2 us -> none  [shards(): gain_sum = lax.psum(kept_five[-1] + kept_six[-1], 'dp')]
    pallas_call x7, Pallas kernels: 87.2 us -> 103 us  [the longest x6 92.5 us: run_layer(): pl.pallas_call(kernel, out_shape=list(outs.values()), in_specs=[specs.get...]
    unnamed x99 -> x32, local copies, waits for them, and re-layouts: 25.4 us -> 9.55 us
    ppermute x0 -> x14, starting transfers between devices: none -> 15.4 us  [the longest x6 6.56 us: moved(): lax.ppermute(value, 'dp', [(place_of(z, x, c), place_of(z ^ dz, x ^ dx, c...]
  transfers between devices with their start and end apart: 6 -> 19, of which waited for: 4 -> 14; matrix products, arithmetic and copies ran while one was open for 4% -> 4% of each run, Pallas kernels for 7% -> 15%
where the time goes in v2:
time: 321 us; the launch traced here: 316 us
  Pallas kernels  103 us (32%)
  waiting for transfers between devices  76.9 us (24%)
  blocking collectives  56.7 us (18%)
  starting transfers between devices  23.3 us (7%)
  other arithmetic  21 us (7%)
  local copies, waits for them, and re-layouts  19.5 us (6%)
  between operations  14.9 us (5%)
    pallas_call x6, Pallas kernels, run_layer(): pl.pallas_call(kernel, out_shape=list(outs.values()), in_specs=[specs.get...  92.5 us
    all_gather x1, blocking collectives, gather_weights(): c_lo = lax.all_gather(w_down[:EACH_FF // 2], 'dp', axis=0, tiled=False)  29.4 us
    all_gather x1, blocking collectives, gather_weights(): c_hi = lax.all_gather(w_down[EACH_FF // 2:], 'dp', axis=0, tiled=False)  27.4 us
    ppermute x3, waiting for transfers between devices, to_far(): lax.ppermute(block, 'dp', [(place_of(z, x, c), place_of((z + far) % 4, x,...  25.1 us
    ppermute x4, waiting for transfers between devices, to_across(): lax.ppermute(block, 'dp', [(place_of(z, x, c), place_of(z, 1 - x, c)) for...  23.6 us
    pallas_call x1, Pallas kernels, run_weights(): pl.pallas_call(kernel, out_shape=list(outs.values()), in_specs=[SMEM] + [...  10.9 us
    all_gather x1, waiting for transfers between devices, gather_weights(): agu = lax.all_gather(packed, 'dp', axis=1, tiled=True)  10.7 us
    ppermute x2, waiting for transfers between devices, send_back(): return lax.ppermute(block, 'section', [(1, 0)])  10.4 us
  transfers between devices with their start and end apart: 19, of which 14 were waited for; matrix products, arithmetic and copies ran while one was open for 4% of the time, Pallas kernels for 15%

profile of v2, /device:TPU:0, one launch (start us, length us, event | category | flops | bytes accessed | tf_op | source)
XLA Modules:
  0.0 315.7 jit_solution(8465469699701585920)
XLA Ops:
  23.8 29.4 %all_gather.17.refs_5_ = bf16[16,48,576]{2,1,0:T(8,128)(2,1)} all-gather(bf16[1,48,576]{2,1,0:T(8,128)(2,1)S(1)} %all_gather.16), channel_id=1, replica_groups=mesh['section'=2,'dp'=16] {'dp'}, dimensions={0}, use_global_device_ids=true | all-gather | bytes 940032 | tf_op jit(solution)/shard_map/all_gather | solution.py:585
  53.2 27.4 %all_gather.19.refs_6_ = bf16[16,48,576]{2,1,0:T(8,128)(2,1)} all-gather(bf16[1,48,576]{2,1,0:T(8,128)(2,1)S(1)} %all_gather.18), channel_id=1, replica_groups=mesh['section'=2,'dp'=16] {'dp'}, dimensions={0}, use_global_device_ids=true | all-gather | bytes 940032 | tf_op jit(solution)/shard_map/all_gather | solution.py:586
  80.5 10.7 %all-gather.2.cloned.1.call-done.refs_4_ = bf16[3,640,1536]{2,1,0:T(8,128)(2,1)} async-done(((bf16[3,40,1536]{2,1,0:T(8,128)(2,1)}), bf16[3,640,1536]{2,1,0:T(8,128)(2,1)}) %all-gather.2.cloned.1.call-update) | async-done | bytes 5898256 | tf_op jit(solution)/shard_map/all_gather | solution.py:583
  92.3 11.2 %layer_lead.3 = bf16[256,576]{1,0:T(8,128)(2,1)} custom-call(s32[8]{0:T(128)} %stack.45.refs_0_, bf16[2,256,576]{2,1,0:T(8,128)(2,1)} %copy.49.refs_1_, f32[1,576]{1,0:T(1,128)} %refs_2_.11, f32[1,576]{1,0:T(1,128)} %refs_3_.11, bf16[3,640,1536]{2,1,0:T(8,128)(2,1)} %all-gather.2.cloned.1.call-done.refs_4_, bf16[16,48,576]{2,1,0:T(8,128)(2,1)} %all_gather.17.refs_5_, ...), custom_call_target="tpu_custom_call" | custom-call | tf_op jit(solution)/shard_map/layer_lead/pallas_call | solution.py:447
  103.5 3.5 %collective-permute-start.1 = (bf16[256,576]{1,0:T(8,128)(2,1)}, bf16[256,576]{1,0:T(8,128)(2,1)S(1)}, u32[]{:S(2)}, u32[]{:S(2)}) collective-permute-start(bf16[256,576]{1,0:T(8,128)(2,1)} %layer_lead.3), channel_id=1, source_target_pairs={{0,16},{1,17},{2,18},{3,19},{4,20},{5,21},{6,22},{7,23},{8,24},{9,... | collective-permute-start | bytes 884744 | tf_op jit(solution)/shard_map/ppermute | solution.py:701
  107.0 11.2 %layer_lead.2 = bf16[256,576]{1,0:T(8,128)(2,1)} custom-call(s32[8]{0:T(128)} %stack.45.refs_0_, bf16[2,256,576]{2,1,0:T(8,128)(2,1)} %copy.49.refs_1_, f32[1,576]{1,0:T(1,128)} %refs_2_.11, f32[1,576]{1,0:T(1,128)} %refs_3_.11, bf16[3,640,1536]{2,1,0:T(8,128)(2,1)} %all-gather.2.cloned.1.call-done.refs_4_, bf16[16,48,576]{2,1,0:T(8,128)(2,1)} %all_gather.17.refs_5_, ...), custom_call_target="tpu_custom_call" | custom-call | tf_op jit(solution)/shard_map/layer_lead/pallas_call | solution.py:447
  121.8 22.8 %layer_both.1 = (bf16[256,576]{1,0:T(8,128)(2,1)}, bf16[256,576]{1,0:T(8,128)(2,1)}, bf16[256,640]{1,0:T(8,128)(2,1)}, bf16[256,768]{1,0:T(8,128)(2,1)}, bf16[25...) custom-call(s32[8]{0:T(128)} %stack.45.refs_0_, ...), custom_call_target="tpu_custom_call" | custom-call | tf_op jit(solution)/shard_map/layer_both/pallas_call | solution.py:447
  146.7 12.6 %layer_ahead.1 = (bf16[256,576]{1,0:T(8,128)(2,1)}, bf16[256,640]{1,0:T(8,128)(2,1)}, bf16[256,768]{1,0:T(8,128)(2,1)}, bf16[256,192]{1,0:T(8,128)(2,1)}, f32[25...) custom-call(s32[8]{0:T(128)} %stack.45.refs_0_, ...), custom_call_target="tpu_custom_call" | custom-call | tf_op jit(solution)/shard_map/layer_ahead/pallas_call | solution.py:447
  160.1 17.5 %layer_behind.2 = (bf16[256,576]{1,0:T(8,128)(2,1)}, f32[2,576]{1,0:T(2,128)}, bf16[256,768]{1,0:T(8,128)(2,1)}, bf16[256,256]{1,0:T(8,128)(2,1)}, bf16[256,576]...) custom-call(s32[8]{0:T(128)} %stack.45.refs_0_, bf16[2,256,576]{2,1,0:T(8,128)(2,1)} %copy.49.refs_1_, ...), custom_call_target="tpu_custom_call" | custom-call | tf_op jit(solution)/shard_map/layer_behind/pallas_call | solution.py:447
  178.9 10.4 %collective-permute-done.3.refs_13_.refs_12_ = bf16[256,576]{1,0:T(8,128)(2,1)S(1)} collective-permute-done((bf16[256,576]{1,0:T(8,128)(2,1)}, bf16[256,576]{1,0:T(8,128)(2,1)S(1)}, u32[]{:S(2)}, u32[]{:S(2)}) %collective-permute-start.3) | collective-permute-done | bytes 294944 | tf_op jit(solution)/shard_map/ppermute | solution.py:704
  190.1 17.3 %layer_behind.3 = (bf16[256,576]{1,0:T(8,128)(2,1)}, f32[2,576]{1,0:T(2,128)}, bf16[256,768]{1,0:T(8,128)(2,1)}, bf16[256,256]{1,0:T(8,128)(2,1)}, bf16[256,576]...) custom-call(s32[8]{0:T(128)} %stack.45.refs_0_, bf16[2,256,576]{2,1,0:T(8,128)(2,1)} %copy.49.refs_1_, ...), custom_call_target="tpu_custom_call" | custom-call | tf_op jit(solution)/shard_map/layer_behind/pallas_call | solution.py:447
  207.4 10.9 %weight_grads.1 = (bf16[2,4,4,40,1536]{4,3,2,1,0:T(8,128)(2,1)}, bf16[2,4,4,40,1536]{4,3,2,1,0:T(8,128)(2,1)}) custom-call(s32[8]{0:T(128)} %stack.45.refs_0_, bf16[2,256,576]{2,1,0:T(8,128)(2,1)} %copy.52.refs_12_.refs_1_, bf16[256,576]{1,0:T(8,128)(2,1)} %copy-done.2, bf16[256,1536]{1,0:T(8,128)(2,1)} %get-tuple-element.100.refs_3_, ...), custom_call_target="tpu_custom_call" | custom-call | tf_op jit(solution)/shard_map/weight_grads/pallas_call | solution.py:541
  222.5 2.6 collective-permute-done.5
  227.2 2.1 fusion.12
  231.4 2.0 collective-permute-start.13
  237.9 5.4 %collective-permute-done.10 = bf16[4,40,1536]{2,1,0:T(8,128)(2,1)S(1)} collective-permute-done((bf16[4,40,1536]{2,1,0:T(8,128)(2,1)S(1)}, bf16[4,40,1536]{2,1,0:T(8,128)(2,1)S(1)}, u32[]{:S(2)}, u32[]{:S(2)}) %collective-permute-start.10) | collective-permute-done | bytes 491552 | tf_op jit(solution)/shard_map/ppermute | solution.py:615
  243.4 9.8 %collective-permute-done.8 = bf16[4,40,1536]{2,1,0:T(8,128)(2,1)} collective-permute-done((bf16[4,40,1536]{2,1,0:T(8,128)(2,1)S(1)}, bf16[4,40,1536]{2,1,0:T(8,128)(2,1)}, u32[]{:S(2)}, u32[]{:S(2)}) %collective-permute-start.8) | collective-permute-done | bytes 491552 | tf_op jit(solution)/shard_map/ppermute | solution.py:615
  253.2 2.0 fusion.3
  257.0 2.1 collective-permute-start.14
  261.2 8.3 %collective-permute-done.16 = bf16[4,40,1536]{2,1,0:T(8,128)(2,1)} collective-permute-done((bf16[4,40,1536]{2,1,0:T(8,128)(2,1)S(1)}, bf16[4,40,1536]{2,1,0:T(8,128)(2,1)}, u32[]{:S(2)}, u32[]{:S(2)}) %collective-permute-start.16) | collective-permute-done | bytes 491552 | tf_op jit(solution)/shard_map/ppermute | solution.py:615
  269.5 2.3 fusion.1
  271.8 2.0 collective-permute-start.17
  275.6 16.8 %collective-permute-done.14 = bf16[4,40,1536]{2,1,0:T(8,128)(2,1)S(1)} collective-permute-done((bf16[4,40,1536]{2,1,0:T(8,128)(2,1)S(1)}, bf16[4,40,1536]{2,1,0:T(8,128)(2,1)S(1)}, u32[]{:S(2)}, u32[]{:S(2)}) %collective-permute-start.14) | collective-permute-done | bytes 491552 | tf_op jit(solution)/shard_map/ppermute | solution.py:619
  292.4 8.3 %collective-permute-done.17 = bf16[4,40,1536]{2,1,0:T(8,128)(2,1)S(1)} collective-permute-done((bf16[4,40,1536]{2,1,0:T(8,128)(2,1)}, bf16[4,40,1536]{2,1,0:T(8,128)(2,1)S(1)}, u32[]{:S(2)}, u32[]{:S(2)}) %collective-permute-start.17) | collective-permute-done | bytes 491552 | tf_op jit(solution)/shard_map/ppermute | solution.py:619
  (107 shorter events, 52.2 us)
Async XLA Ops:
  7.2 84.1 %all-gather.2.cloned.1.call-start = ((), (), s32[]{:S(2)}) async-start(), calls=%async_computation | async-start | bytes 6266880 | tf_op jit(solution)/shard_map/all_gather | solution.py:583
  14.9 76.3 %copy-start.5 = (bf16[2,256,576]{1,2,0:T(8,128)(2,1)S(1)}, bf16[2,256,576]{1,2,0:T(8,128)(2,1)}, u32[]{:S(2)}) copy-start(bf16[2,256,576]{1,2,0:T(8,128)(2,1)} %param.12) | copy-start | bytes 1769476
  103.5 16.5 %copy-start.6 = (bf16[2,256,576]{1,2,0:T(8,128)(2,1)S(1)}, bf16[2,256,576]{1,2,0:T(8,128)(2,1)}, u32[]{:S(2)}) copy-start(bf16[2,256,576]{1,2,0:T(8,128)(2,1)} %param.23) | copy-start | bytes 1769476
  103.5 17.6 %collective-permute-start.1 = (bf16[256,576]{1,0:T(8,128)(2,1)}, bf16[256,576]{1,0:T(8,128)(2,1)S(1)}, u32[]{:S(2)}, u32[]{:S(2)}) collective-permute-start(bf16[256,576]{1,0:T(8,128)(2,1)} %layer_lead.3), channel_id=1, source_target_pairs={{0,16},{1,17},{2,18},{3,19},{4,20},{5,21},{6,22},{7,23},{8,24},{9,... | collective-permute-start | bytes 884744 | tf_op jit(solution)/shard_map/ppermute | solution.py:701
  118.2 27.7 %collective-permute-start = (bf16[256,576]{1,0:T(8,128)(2,1)}, bf16[256,576]{1,0:T(8,128)(2,1)S(1)}, u32[]{:S(2)}, u32[]{:S(2)}) collective-permute-start(bf16[256,576]{1,0:T(8,128)(2,1)} %layer_lead.2), channel_id=1, source_target_pairs={{0,16},{1,17},{2,18},{3,19},{4,20},{5,21},{6,22},{7,23},{8,24},{9,... | collective-permute-start | bytes 884744 | tf_op jit(solution)/shard_map/ppermute | solution.py:701
  144.6 14.7 %collective-permute-start.2 = (bf16[256,576]{1,0:T(8,128)(2,1)}, bf16[256,576]{1,0:T(8,128)(2,1)S(1)}, u32[]{:S(2)}, u32[]{:S(2)}) collective-permute-start(bf16[256,576]{1,0:T(8,128)(2,1)} %get-tuple-element.85), channel_id=1, source_target_pairs={{16,0},{17,1},{18,2},{19,3},{20,4},{21,5},{22,6},{23,7},{24,8},{25... | collective-permute-start | bytes 884744 | tf_op jit(solution)/shard_map/ppermute | solution.py:704
  177.6 11.7 %collective-permute-start.3 = (bf16[256,576]{1,0:T(8,128)(2,1)}, bf16[256,576]{1,0:T(8,128)(2,1)S(1)}, u32[]{:S(2)}, u32[]{:S(2)}) collective-permute-start(bf16[256,576]{1,0:T(8,128)(2,1)} %get-tuple-element.92), channel_id=1, source_target_pairs={{16,0},{17,1},{18,2},{19,3},{20,4},{21,5},{22,6},{23,7},{24,8},{25... | collective-permute-start | bytes 884744 | tf_op jit(solution)/shard_map/ppermute | solution.py:704
  218.2 7.1 %collective-permute-start.4 = (bf16[2,4,4,40,1536]{4,3,2,1,0:T(8,128)(2,1)}, bf16[2,4,4,40,1536]{4,3,2,1,0:T(8,128)(2,1)S(1)}, u32[]{:S(2)}, u32[]{:S(2)}) collective-permute-start(bf16[2,4,4,40,1536]{4,3,2,1,0:T(8,128)(2,1)} %get-tuple-element.119), channel_id=1, source_target_pairs={{0,1},{1,0},{2,3},{3,2},{4,5},{5,4},{6,7},{7,6},{8,9},{9,8},{10,11... | collective-permute-start | bytes 11796488 | tf_op jit(solution)/shard_map/ppermute | solution.py:611
  218.4 3.1 collective-permute-start.7
  218.9 3.6 %collective-permute-start.6 = (f32[2,576]{1,0:T(2,128)S(1)}, f32[2,576]{1,0:T(2,128)S(1)}, u32[]{:S(2)}, u32[]{:S(2)}) collective-permute-start(f32[2,576]{1,0:T(2,128)S(1)} %add.101), channel_id=1, source_target_pairs={{0,2},{1,3},{2,0},{3,1},{4,6},{5,7},{6,4},{7,5},{8,10},{9,11},{10,... | collective-permute-start | bytes 13832 | tf_op jit(solution)/shard_map/ppermute | solution.py:627
  220.5 4.6 %collective-permute-start.5 = (f32[2,576]{1,0:T(2,128)S(1)}, f32[2,576]{1,0:T(2,128)S(1)}, u32[]{:S(2)}, u32[]{:S(2)}) collective-permute-start(f32[2,576]{1,0:T(2,128)S(1)} %add.101), channel_id=1, source_target_pairs={{0,1},{1,0},{2,3},{3,2},{4,5},{5,4},{6,7},{7,6},{8,9},{9,8},{10,11... | collective-permute-start | bytes 13832 | tf_op jit(solution)/shard_map/ppermute | solution.py:627
  227.2 28.5 %copy-start.7 = (bf16[256,576]{1,0:T(8,128)(2,1)S(1)}, bf16[256,576]{1,0:T(8,128)(2,1)}, u32[]{:S(2)}) copy-start(bf16[256,576]{1,0:T(8,128)(2,1)} %get-tuple-element.84) | copy-start | bytes 884740
  227.2 28.5 %copy-start.8 = (bf16[256,576]{1,0:T(8,128)(2,1)S(1)}, bf16[256,576]{1,0:T(8,128)(2,1)}, u32[]{:S(2)}) copy-start(bf16[256,576]{1,0:T(8,128)(2,1)} %get-tuple-element.82) | copy-start | bytes 884740
  229.2 27.6 %copy-start.9 = (bf16[256,576]{1,0:T(8,128)(2,1)S(1)}, bf16[256,576]{1,0:T(8,128)(2,1)}, u32[]{:S(2)}) copy-start(bf16[256,576]{1,0:T(8,128)(2,1)} %get-tuple-element.92) | copy-start | bytes 884740
  229.3 14.1 %collective-permute-start.10 = (bf16[4,40,1536]{2,1,0:T(8,128)(2,1)S(1)}, bf16[4,40,1536]{2,1,0:T(8,128)(2,1)S(1)}, u32[]{:S(2)}, u32[]{:S(2)}) collective-permute-start(bf16[4,40,1536]{2,1,0:T(8,128)(2,1)S(1)} %get-tuple-element.172), channel_id=1, source_target_pairs={{0,2},{1,3},{2,0},{3,1},{4,6},{5,7},{6,4},{7,5},{8,10},{9,11},{10,... | collective-permute-start | bytes 1474568 | tf_op jit(solution)/shard_map/ppermute | solution.py:615
  229.7 23.5 %collective-permute-start.8 = (bf16[4,40,1536]{2,1,0:T(8,128)(2,1)S(1)}, bf16[4,40,1536]{2,1,0:T(8,128)(2,1)}, u32[]{:S(2)}, u32[]{:S(2)}) collective-permute-start(bf16[4,40,1536]{2,1,0:T(8,128)(2,1)S(1)} %get-tuple-element.173), channel_id=1, source_target_pairs={{0,2},{1,3},{2,0},{3,1},{4,6},{5,7},{6,4},{7,5},{8,10},{9,11},{10,... | collective-permute-start | bytes 1474568 | tf_op jit(solution)/shard_map/ppermute | solution.py:615
  231.4 5.4 %collective-permute-start.13 = (f32[2,576]{1,0:T(2,128)S(1)}, f32[2,576]{1,0:T(2,128)S(1)}, u32[]{:S(2)}, u32[]{:S(2)}) collective-permute-start(f32[2,576]{1,0:T(2,128)S(1)} %add_add_fusion.1), channel_id=1, source_target_pairs={{0,12},{1,13},{2,14},{3,15},{4,8},{5,9},{6,10},{7,11},{8,4},{9,5},... | collective-permute-start | bytes 13832 | tf_op jit(solution)/shard_map/ppermute | solution.py:627
  233.3 4.5 %collective-permute-start.12 = (f32[2,576]{1,0:T(2,128)S(1)}, f32[2,576]{1,0:T(2,128)S(1)}, u32[]{:S(2)}, u32[]{:S(2)}) collective-permute-start(f32[2,576]{1,0:T(2,128)S(1)} %add_add_fusion.1), channel_id=1, source_target_pairs={{0,8},{1,9},{2,10},{3,11},{4,12},{5,13},{6,14},{7,15},{8,0},{9,1},... | collective-permute-start | bytes 13832 | tf_op jit(solution)/shard_map/ppermute | solution.py:627
  234.3 3.6 %collective-permute-start.11 = (f32[2,576]{1,0:T(2,128)S(1)}, f32[2,576]{1,0:T(2,128)S(1)}, u32[]{:S(2)}, u32[]{:S(2)}) collective-permute-start(f32[2,576]{1,0:T(2,128)S(1)} %add_add_fusion.1), channel_id=1, source_target_pairs={{0,4},{1,5},{2,6},{3,7},{4,0},{5,1},{6,2},{7,3},{8,12},{9,13},{10,... | collective-permute-start | bytes 13832 | tf_op jit(solution)/shard_map/ppermute | solution.py:627
  255.2 14.3 %collective-permute-start.16 = (bf16[4,40,1536]{2,1,0:T(8,128)(2,1)S(1)}, bf16[4,40,1536]{2,1,0:T(8,128)(2,1)}, u32[]{:S(2)}, u32[]{:S(2)}) collective-permute-start(bf16[4,40,1536]{2,1,0:T(8,128)(2,1)S(1)} %get-tuple-element.130), channel_id=1, source_target_pairs={{0,2},{1,3},{2,0},{3,1},{4,6},{5,7},{6,4},{7,5},{8,10},{9,11},{10,... | collective-permute-start | bytes 1474568 | tf_op jit(solution)/shard_map/ppermute | solution.py:615
  257.0 35.5 %collective-permute-start.14 = (bf16[4,40,1536]{2,1,0:T(8,128)(2,1)S(1)}, bf16[4,40,1536]{2,1,0:T(8,128)(2,1)S(1)}, u32[]{:S(2)}, u32[]{:S(2)}) collective-permute-start(bf16[4,40,1536]{2,1,0:T(8,128)(2,1)S(1)} %get-tuple-element.128), channel_id=1, source_target_pairs={{0,8},{1,9},{2,10},{3,11},{4,12},{5,13},{6,14},{7,15},{8,0},{9,1},... | collective-permute-start | bytes 1474568 | tf_op jit(solution)/shard_map/ppermute | solution.py:619
  259.1 33.3 %collective-permute-start.9 = (bf16[4,40,1536]{2,1,0:T(8,128)(2,1)S(1)}, bf16[4,40,1536]{2,1,0:T(8,128)(2,1)}, u32[]{:S(2)}, u32[]{:S(2)}) collective-permute-start(bf16[4,40,1536]{2,1,0:T(8,128)(2,1)S(1)} %get-tuple-element.123), channel_id=1, source_target_pairs={{0,2},{1,3},{2,0},{3,1},{4,6},{5,7},{6,4},{7,5},{8,10},{9,11},{10,... | collective-permute-start | bytes 1474568 | tf_op jit(solution)/shard_map/ppermute | solution.py:615
  260.6 31.8 %collective-permute-start.15 = (bf16[4,40,1536]{2,1,0:T(8,128)(2,1)S(1)}, bf16[4,40,1536]{2,1,0:T(8,128)(2,1)}, u32[]{:S(2)}, u32[]{:S(2)}) collective-permute-start(bf16[4,40,1536]{2,1,0:T(8,128)(2,1)S(1)} %get-tuple-element.129), channel_id=1, source_target_pairs={{0,4},{1,5},{2,6},{3,7},{4,8},{5,9},{6,10},{7,11},{8,12},{9,13},{1... | collective-permute-start | bytes 1474568 | tf_op jit(solution)/shard_map/ppermute | solution.py:619
  271.8 28.9 %collective-permute-start.17 = (bf16[4,40,1536]{2,1,0:T(8,128)(2,1)}, bf16[4,40,1536]{2,1,0:T(8,128)(2,1)S(1)}, u32[]{:S(2)}, u32[]{:S(2)}) collective-permute-start(bf16[4,40,1536]{2,1,0:T(8,128)(2,1)} %fusion.1), channel_id=1, source_target_pairs={{0,12},{1,13},{2,14},{3,15},{4,0},{5,1},{6,2},{7,3},{8,4},{9,5},{1... | collective-permute-start | bytes 1474568 | tf_op jit(solution)/shard_map/ppermute | solution.py:619
  (8 other events, 28.5 us)
Sparse Core Ops, SparseCore 0:
  16.0 75.2 all-gather.1
